TPU v7x, 32 devices: a whole 2x2x4 slice. The times are simulated.
32 devices in a mesh: dp: 4 (over x, core), seq: 8 (over z, y).
Axes of the slice: x: 2, y: 2, z: 4, core: 2. Of those that a mesh axis runs over, the one named last changes fastest.
Arguments:
- tokens: bfloat16 [4, 16384, 1024], P('dp', 'seq'), may hold values from -6 to 6
- cotangent: bfloat16 [4, 16384, 1024], P('dp', 'seq'), may hold values from -6 to 6
- gain_mix: float32 [1024], replicated, may hold values from 0.25 to 1.75
- gain_mlp: float32 [1024], replicated, may hold values from 0.25 to 1.75
- fine_factor: bfloat16 [8, 128, 128], replicated, may hold values from -3.2 to 3.2, as said below
- coarse_factor: bfloat16 [8, 128, 128], replicated, may hold values from -3.2 to 3.2, as said below
- w_gate_up: bfloat16 [1024, 2048], P(('dp', 'seq')), may hold values from -0.1875 to 0.1875
- w_down: bfloat16 [1024, 1024], P(('dp', 'seq')), may hold values from -0.1875 to 0.1875
Outputs:
- layer_out: bfloat16 [4, 16384, 1024], P('dp', 'seq')
- grad_input: bfloat16 [4, 16384, 1024], P('dp', 'seq')
- grad_gate_up: float32 [1024, 2048], P(('dp', 'seq'))
- grad_down: float32 [1024, 1024], P(('dp', 'seq'))
- grad_fine: float32 [8, 128, 128], replicated
- grad_coarse: float32 [8, 128, 128], replicated
- grad_gain_mix: float32 [1024], replicated
- grad_gain_mlp: float32 [1024], replicated
Inputs may be any that keep to these rules, and one draw needn't show every extreme that they name: `fine_factor`: each group's factor is lower triangular: entries above the diagonal are zero. `coarse_factor`: each group's factor is lower triangular: entries above the diagonal are zero.
All inputs are finite; a program needn't handle non-finite values.
Results may differ from a plain program's by a relative error of at most 0.012.
Values may be sent and summed in bfloat16 or wider, within the bound.
No kernel may reach another device: no remote copies, remote signals or barrier semaphores. Data moves between devices by JAX's collectives and lax.ppermute only.
A program may use at most 192 MiB of HBM per device.

v0:
```python
import math

import jax
import jax.numpy as jnp
from jax import lax
from jax.sharding import PartitionSpec as P

D = 1024
FF = 1024
NB = 128
NC = 128
GW = 128


epsilon = 1e-05


def widen(values):
    return lax.optimization_barrier(values).astype(jnp.float32)


def norm_rows(values):
    scale_inv = lax.rsqrt(jnp.mean(values * values, axis=-1, keepdims=True) + epsilon)
    return (values * scale_inv, scale_inv)


def norm_back(upstream, normed, scale_inv):
    return scale_inv * (upstream - normed * jnp.mean(upstream * normed, axis=-1, keepdims=True))


def silu_parts(gate_pre):
    squash = jax.nn.sigmoid(gate_pre)
    return (gate_pre * squash, squash * (1.0 + gate_pre * (1.0 - squash)))


def into_coarse(block_data):
    return lax.all_to_all(block_data, "seq", split_axis=1, concat_axis=0, tiled=True)


def into_fine(block_data):
    return lax.all_to_all(block_data, "seq", split_axis=0, concat_axis=1, tiled=True)


def on_device(tokens, cotangent, gain_mix, gain_mlp, fine_factor, coarse_factor, w_gate_up, w_down):
    groups = D // GW
    local_rows = tokens.shape[1]
    block_count = local_rows // NB
    seq_devices = lax.axis_size("seq")
    data_devices = lax.axis_size("dp")
    fine_width = NB // seq_devices
    full_gate_up, full_down = (
        lax.all_gather(w_gate_up, ("dp", "seq"), axis=0, tiled=True),
        lax.all_gather(w_down, ("dp", "seq"), axis=0, tiled=True),
    )
    source = tokens[0].astype(jnp.float32)
    normed_mix, inv_mix = norm_rows(source)
    hidden_in = (normed_mix * gain_mix).astype(jnp.bfloat16)
    gated_in = widen(hidden_in)
    blocked = hidden_in.reshape(block_count, NB, groups, GW)
    fine_mixed = jnp.einsum(
        "gpq,aqgc->apgc", fine_factor, blocked, preferred_element_type=jnp.float32
    ).astype(jnp.bfloat16)
    fine_moved = into_coarse(fine_mixed.reshape(block_count, NB, D)).reshape(
        NC, fine_width, groups, GW
    )
    coarse_mixed = jnp.einsum(
        "gpq,qbgc->pbgc", coarse_factor, fine_moved, preferred_element_type=jnp.float32
    ).astype(jnp.bfloat16)
    mixed = widen(into_fine(coarse_mixed.reshape(NC, fine_width, D))).reshape(local_rows, D)
    after_mix = source + mixed * gated_in
    normed_mlp, inv_mlp = norm_rows(after_mix)
    mlp_in = (normed_mlp * gain_mlp).astype(jnp.bfloat16)
    both = jnp.dot(mlp_in, full_gate_up, preferred_element_type=jnp.float32)
    gate_pre = both[:, :FF]
    upward = both[:, FF:]
    silu_gate, silu_slope = silu_parts(gate_pre)
    activation = (silu_gate * upward).astype(jnp.bfloat16)
    projected = lax.dot_general(
        activation, full_down, (((1,), (1,)), ((), ())), preferred_element_type=jnp.float32
    )
    layer = (after_mix + projected).astype(jnp.bfloat16)
    upstream_out = cotangent[0]
    upstream = upstream_out.astype(jnp.float32)
    back_act = widen(
        jnp.dot(upstream_out, full_down, preferred_element_type=jnp.float32).astype(jnp.bfloat16)
    )
    back_both = jnp.concatenate(
        [back_act * upward * silu_slope, back_act * silu_gate], axis=1
    ).astype(jnp.bfloat16)
    gate_up_part = lax.dot_general(
        mlp_in, back_both, (((0,), (0,)), ((), ())), preferred_element_type=jnp.float32
    )
    down_part = lax.dot_general(
        upstream_out, activation, (((0,), (0,)), ((), ())), preferred_element_type=jnp.float32
    )
    weight_grads = lax.psum_scatter(
        jnp.concatenate([gate_up_part, down_part], axis=1),
        ("dp", "seq"),
        scatter_dimension=0,
        tiled=True,
    )
    back_mlp_in = lax.dot_general(
        back_both, full_gate_up, (((1,), (1,)), ((), ())), preferred_element_type=jnp.float32
    )
    gain_mlp_term = jnp.sum(back_mlp_in * normed_mlp, axis=0)
    back_after = upstream + norm_back(back_mlp_in * gain_mlp, normed_mlp, inv_mlp)
    back_mixed = (back_after * gated_in).astype(jnp.bfloat16)
    mixed_moved = into_coarse(back_mixed.reshape(block_count, NB, D)).reshape(
        NC, fine_width, groups, GW
    )
    back_fine_moved = jnp.einsum(
        "gpq,pbgc->qbgc", coarse_factor, mixed_moved, preferred_element_type=jnp.float32
    ).astype(jnp.bfloat16)
    coarse_term = jnp.einsum(
        "pbgc,qbgc->gpq", mixed_moved, fine_moved, preferred_element_type=jnp.float32
    )
    back_fine = into_fine(back_fine_moved.reshape(NC, fine_width, D)).reshape(
        block_count, NB, groups, GW
    )
    back_blocked = jnp.einsum(
        "gpq,apgc->aqgc", fine_factor, back_fine, preferred_element_type=jnp.float32
    ).reshape(local_rows, D)
    fine_term = jnp.einsum("apgc,aqgc->gpq", back_fine, blocked, preferred_element_type=jnp.float32)
    back_hidden = back_after * mixed + back_blocked
    gain_mix_term = jnp.sum(back_hidden * normed_mix, axis=0)
    grad_in = (back_after + norm_back(back_hidden * gain_mix, normed_mix, inv_mix)).astype(
        jnp.bfloat16
    )
    summed = lax.psum((fine_term, coarse_term, gain_mix_term, gain_mlp_term), ("dp", "seq"))
    all_seqs = data_devices * tokens.shape[0]
    scale_tokens = 1.0 / math.sqrt(all_seqs * NC * NB)
    grad_fine = jnp.tril(summed[0]) * (1.0 / math.sqrt(all_seqs * NC * GW))
    grad_coarse = jnp.tril(summed[1]) * (1.0 / math.sqrt(all_seqs * NB * GW))
    grad_gate_up = weight_grads[:, : 2 * FF] * scale_tokens
    grad_down = weight_grads[:, 2 * FF :] * scale_tokens
    return (
        layer.reshape(1, local_rows, D),
        grad_in.reshape(1, local_rows, D),
        grad_gate_up,
        grad_down,
        grad_fine,
        grad_coarse,
        summed[2] * scale_tokens,
        summed[3] * scale_tokens,
    )


def solution(mesh):
    placed = (
        P("dp", "seq", None),
        P("dp", "seq", None),
        P(),
        P(),
        P(),
        P(),
        P(("dp", "seq"), None),
        P(("dp", "seq"), None),
    )
    return jax.shard_map(
        on_device,
        mesh=mesh,
        in_specs=placed,
        out_specs=(
            P("dp", "seq", None),
            P("dp", "seq", None),
            P(("dp", "seq"), None),
            P(("dp", "seq"), None),
            P(),
            P(),
            P(),
            P(),
        ),
        check_vma=False,
    )
```

profile of v0, /device:TPU:0, one launch (start us, length us, event | category | flops | bytes accessed | tf_op | source)
XLA Modules:
  0.0 861.4 jit_solution(12585245093300385873)
XLA Ops:
  21.3 6.7 copy.65
  28.0 7.3 all-to-all-start
  36.0 96.8 %all-to-all-done = bf16[16,128,1024]{2,0,1:T(8,128)(2,1)} async-done(((bf16[16,128,1024]{2,0,1:T(8,128)(2,1)}), bf16[16,128,1024]{2,0,1:T(8,128)(2,1)}, u32[]{:S(2)}, u32[]{:S(2)}) %all-to-all-start) | async-done | bytes 4194336 | tf_op jit(solution)/shard_map/all_to_all | solution.py:37
  145.9 6.7 copy.70
  162.2 9.4 %fusion.31 = bf16[2048,1024]{0,1:T(8,128)(2,1)} fusion(bf16[1024,1024]{1,0:T(8,128)(2,1)} %all-gather.5.cloned.1.call-done, bf16[1,2048,1024]{2,1,0:T(8,128)(2,1)} %param.9), kind=kOutput, calls=%fused_computation.52 | convolution fusion | flops 4297064448 | bytes 10485760 | tf_op jit(solution)/shard_map/dot_general | solution.py:85
  171.6 86.6 %all-to-all-done.1 = bf16[128,16,1024]{2,1,0:T(8,128)(2,1)} async-done(((bf16[128,16,1024]{2,1,0:T(8,128)(2,1)}), bf16[128,16,1024]{2,1,0:T(8,128)(2,1)}, u32[]{:S(2)}, u32[]{:S(2)}) %all-to-all-start.1) | async-done | bytes 4194336 | tf_op jit(solution)/shard_map/all_to_all | solution.py:41
  269.0 12.3 %all-gather.3.cloned.1.call-done = bf16[1024,2048]{1,0:T(8,128)(2,1)} async-done(((bf16[32,2048]{1,0:T(8,128)(2,1)}), bf16[1024,2048]{1,0:T(8,128)(2,1)}) %all-gather.3.cloned.1.call-update) | async-done | bytes 4194320 | tf_op jit(solution)/shard_map/all_gather | solution.py:52
  281.3 16.1 %fusion.72 = f32[2048,2048]{0,1:T(8,128)} fusion(bf16[1024,2048]{1,0:T(8,128)(2,1)} %all-gather.3.cloned.1.call-done, f32[2048,1024]{1,0:T(8,128)} %get-tuple-element.19, f32[1024]{0:T(1024)S(1)} %copy-done.22, f32[2048]{0:T(1024)S(1)} %add_rsqrt_fusion), kind=kOutput, calls=%fused_computation.86 | convolution fusion | flops 8596226048 | bytes 29372416 | tf_op jit(solution)/shard_map/dot_general | solution.py:73
  297.5 12.6 %fusion.9 = (bf16[2048,1024]{0,1:T(8,128)(2,1)}, bf16[2048,1024]{0,1:T(8,128)(2,1)}, bf16[2048,1024]{0,1:T(8,128)(2,1)}) fusion(bf16[2048,1024]{0,1:T(8,128)(2,1)S(1)} %copy-done.14, f32[2048,2048]{0,1:T(8,128)} %fusion.72), kind=kLoop, calls=%fused_computation.17 | loop fusion | flops 33554432 | bytes 33554432 | tf_op jit(solution)/shard_map/convert.3
  310.0 17.9 %multiply_reduce_fusion = (f32[1024]{0:T(1024)S(1)}, f32[2048]{0:T(1024)S(1)}, f32[2048,1024]{1,0:T(8,128)}) fusion(f32[2048,1024]{1,0:T(8,128)} %get-tuple-element.19, f32[2048]{0:T(1024)S(1)} %add_rsqrt_fusion, f32[1024]{0:T(1024)S(1)} %copy-done.22, bf16[1024,2048]{1,0:T(8,128)(2,1)} %all-gather.3.cloned.1.call-done, ...), kind=kOutput, calls=%fused_computation.32 | convolution fusion | flops 8619291648 | bytes 29384704 | tf_op jit(solution)/shard_map/dot_general | solution.py:102
  328.0 9.8 %fusion.7 = (bf16[2048,1024]{1,0:T(8,128)(2,1)S(1)}, f32[2048,1024]{1,0:T(8,128)}) fusion(bf16[2048,1024]{1,0:T(8,128)(2,1)S(1)} %copy-done.8, f32[2048]{0:T(1024)S(1)} %broadcast_multiply_fusion.1, f32[2048,1024]{1,0:T(8,128)} %get-tuple-element.19, f32[2048,1024]{1,0:T(8,128)} %get-tuple-element.27, f32[1024]{0:T(1024)S(1)} %copy-done.22, ...), kind=kLoop, calls=%fused_computation.15 | loop fusion | flops 20971520 | bytes 37769216 | tf_op jit(solution)/shard_map/convert_element_type | solution.py:107
  340.1 97.4 %all_to_all.63 = bf16[16,128,1024]{2,0,1:T(8,128)(2,1)S(1)} all-to-all(bf16[16,128,1024]{2,0,1:T(8,128)(2,1)S(1)} %copy.73), channel_id=1, replica_groups=mesh['dp'=4,'seq'=8] {'seq'}, dimensions={1} | all-to-all | bytes 8388608 | tf_op jit(solution)/shard_map/all_to_all | solution.py:37
  448.6 6.8 copy.78
  460.2 10.0 %fusion.52 = f32[1024,1024]{1,0:T(8,128)} fusion(bf16[2048,1024]{0,1:T(8,128)(2,1)} %get-tuple-element.22, bf16[1,2048,1024]{2,1,0:T(8,128)(2,1)} %param.9), kind=kOutput, calls=%fused_computation.65 | convolution fusion | flops 4294967296 | bytes 12582912 | tf_op jit(solution)/shard_map/dot_general | solution.py:93
  470.2 17.0 %fusion.23 = f32[1024,2048]{1,0:T(8,128)} fusion(bf16[2048,1024]{0,1:T(8,128)(2,1)} %get-tuple-element.21, bf16[2048,1024]{0,1:T(8,128)(2,1)} %get-tuple-element.20, f32[2048,1024]{1,0:T(8,128)} %get-tuple-element.19, f32[1024]{0:T(1024)S(1)} %copy-done.22, f32[2048]{0:T(1024)S(1)} %add_rsqrt_fusion), kind=kOutput, calls=%fused_computation.41 | convolution fusion | flops 8613003264 | bytes 25178112 | tf_op jit(solution)/shard_map/dot_general | solution.py:90
  492.5 60.2 %all-to-all-done.3 = bf16[128,16,1024]{2,1,0:T(8,128)(2,1)} async-done(((bf16[128,16,1024]{2,1,0:T(8,128)(2,1)}), bf16[128,16,1024]{2,1,0:T(8,128)(2,1)}, u32[]{:S(2)}, u32[]{:S(2)}) %all-to-all-start.3) | async-done | bytes 4194336 | tf_op jit(solution)/shard_map/all_to_all | solution.py:41
  561.5 10.7 %pad_maximum_fusion = f32[1024,3072]{1,0:T(8,128)} fusion(f32[1024,1024]{1,0:T(8,128)} %fusion.52, f32[1024,2048]{1,0:T(8,128)} %fusion.23), kind=kLoop, calls=%fused_computation | loop fusion | flops 3145728 | bytes 25165824 | tf_op jit(solution)/shard_map/concatenate | solution.py:97
  572.3 12.1 %fusion.25 = bf16[1,2048,1024]{2,1,0:T(8,128)(2,1)} fusion(f32[2048,1024]{1,0:T(8,128)} %get-tuple-element.19, bf16[2048,1024]{0,1:T(8,128)(2,1)} %get-tuple-element.22, bf16[1024,1024]{1,0:T(8,128)(2,1)} %all-gather.5.cloned.1.call-done), kind=kOutput, calls=%fused_computation.43 | convolution fusion | flops 4299161600 | bytes 18874368 | tf_op jit(solution)/shard_map/dot_general | solution.py:78
  589.1 9.3 %copy.81 = f32[16,128,8,128]{3,2,1,0:T(8,128)} copy(f32[16,128,8,128]{1,3,0,2:T(8,128)} %fusion.45) | data formatting | bytes 16777216 | tf_op jit(solution)/shard_map/gpq,apgc->aqgc/transpose | solution.py:120
  598.4 10.5 %fusion.17 = (f32[1024]{0:T(1024)S(1)}, f32[2048]{0:T(1024)S(1)}) fusion(bf16[1,2048,1024]{2,1,0:T(8,128)(2,1)} %param.8, f32[2048]{0:T(1024)S(1)} %copy-done.21, f32[256,8,8,128]{3,2,1,0:T(8,128)} %bitcast.151, f32[2048,1024]{1,0:T(8,128)} %get-tuple-element.17, bf16[16,128,1024]{2,1,0:T(8,128)(2,1)} %bitcast.154, f32[1024]{0:T(1024)S(1)} %copy-done.19), kind=kLoop, calls=%fused_computation.25 | loop fusion | flops 20968448 | bytes 25190400 | tf_op jit(solution)/shard_map/reduce_sum | solution.py:125
  608.9 38.1 %all-reduce = (f32[1024]{0:T(1024)S(1)}, f32[1024]{0:T(1024)S(1)}) all-reduce(f32[1024]{0:T(1024)S(1)} %get-tuple-element.8, f32[1024]{0:T(1024)S(1)} %get-tuple-element.10), channel_id=1, replica_groups=mesh['dp'=4,'seq'=8] {'dp','seq'}, use_global_device_ids=true, to_apply=%region_8.0 | all-reduce | flops 2048 | bytes 16384 | tf_op jit(solution)/shard_map/psum | solution.py:129
  647.6 12.1 %fusion.26 = bf16[1,2048,1024]{2,1,0:T(8,128)(2,1)} fusion(f32[2048,1024]{1,0:T(8,128)} %get-tuple-element.17, bf16[1,2048,1024]{2,1,0:T(8,128)(2,1)} %param.8, f32[2048]{0:T(1024)S(1)} %broadcast_multiply_fusion, f32[1024]{0:T(1024)S(1)} %copy-done.19, f32[2048]{0:T(1024)S(1)} %copy-done.21, f32[256,8,8,128]{3,2,1,0:T(8,128)} %bitcast.152, ...), kind=kLoop, calls=%fused_computation.44 | loop fusion | flops 23068672 | bytes 29380608 | tf_op jit(solution)/shard_map/reshape | solution.py:138
  659.7 30.2 %all-reduce.4.cloned.1.call-done = (f32[8,128,128]{2,1,0:T(8,128)}, f32[8,128,128]{2,1,0:T(8,128)}) async-done(((f32[8,128,128]{2,1,0:T(8,128)}, f32[8,128,128]{2,1,0:T(8,128)}), (f32[8,128,128]{2,1,0:T(8,128)}, f32[8,128,128]{2,1,0:T(8,128)})) %all-reduce.4.cloned.1.call-update) | async-done | bytes 1048592 | tf_op jit(solution)/shard_map/psum | solution.py:129
  692.2 159.0 %reduce-scatter.2.cloned.1.call-done = f32[32,3072]{1,0:T(8,128)} async-done(((f32[1024,3072]{1,0:T(8,128)}), f32[32,3072]{1,0:T(8,128)}) %reduce-scatter.2.cloned.1.call-update) | async-done | bytes 393232 | tf_op jit(solution)/shard_map/reduce_scatter | solution.py:96
  (93 shorter events, 91.3 us)
Async XLA Ops:
  7.2 131.4 %copy-start = (bf16[8,128,128]{2,1,0:T(8,128)(2,1)S(1)}, bf16[8,128,128]{2,1,0:T(8,128)(2,1)}, u32[]{:S(2)}) copy-start(bf16[8,128,128]{2,1,0:T(8,128)(2,1)} %param.13) | copy-start | bytes 786436
  13.5 144.5 %copy-start.20 = (f32[2048]{0:T(1024)}, f32[2048]{0:T(1024)S(1)}, u32[]{:S(2)}) copy-start(f32[2048]{0:T(1024)S(1)} %get-tuple-element.26) | copy-start | bytes 24580
  28.0 104.8 %all-to-all-start = ((bf16[16,128,1024]{2,0,1:T(8,128)(2,1)}), bf16[16,128,1024]{2,0,1:T(8,128)(2,1)}, u32[]{:S(2)}, u32[]{:S(2)}) async-start(bf16[16,128,1024]{2,0,1:T(8,128)(2,1)} %copy.65), calls=%async_computation | async-start | bytes 8388608 | tf_op jit(solution)/shard_map/all_to_all | solution.py:37
  35.2 126.9 %all-gather.5.cloned.1.call-start = ((), (), s32[]{:S(2)}) async-start(), calls=%async_computation.6 | async-start | bytes 2162688 | tf_op jit(solution)/shard_map/all_gather | solution.py:53
  138.5 7.4 copy-start.9
  152.6 105.5 %all-to-all-start.1 = ((bf16[128,16,1024]{2,1,0:T(8,128)(2,1)}), bf16[128,16,1024]{2,1,0:T(8,128)(2,1)}, u32[]{:S(2)}, u32[]{:S(2)}) async-start(bf16[128,16,1024]{2,1,0:T(8,128)(2,1)} %copy.70), calls=%async_computation.1 | async-start | bytes 8388608 | tf_op jit(solution)/shard_map/all_to_all | solution.py:41
  157.2 124.1 %all-gather.3.cloned.1.call-start = ((), (), s32[]{:S(2)}) async-start(), calls=%async_computation.5 | async-start | bytes 4325376 | tf_op jit(solution)/shard_map/all_gather | solution.py:52
  258.1 6.3 copy-start.7
  261.0 8.0 copy-start.4
  264.5 16.9 %copy-start.22 = (f32[1024]{0:T(1024)S(1)}, f32[1024]{0:T(1024)}, u32[]{:S(2)}) copy-start(f32[1024]{0:T(1024)} %param.11) | copy-start | bytes 12292
  281.3 16.1 %copy-start.14 = (bf16[2048,1024]{0,1:T(8,128)(2,1)S(1)}, bf16[2048,1024]{0,1:T(8,128)(2,1)}, u32[]{:S(2)}) copy-start(bf16[2048,1024]{0,1:T(8,128)(2,1)} %fusion.31) | copy-start | bytes 12582916
  310.0 17.9 %copy-start.8 = (bf16[2048,1024]{1,0:T(8,128)(2,1)S(1)}, bf16[2048,1024]{1,0:T(8,128)(2,1)}, u32[]{:S(2)}) copy-start(bf16[2048,1024]{1,0:T(8,128)(2,1)} %fusion.11) | copy-start | bytes 12582916
  310.0 17.9 %copy-start.13 = (bf16[1,2048,1024]{2,1,0:T(8,128)(2,1)S(1)}, bf16[1,2048,1024]{2,1,0:T(8,128)(2,1)}, u32[]{:S(2)}) copy-start(bf16[1,2048,1024]{2,1,0:T(8,128)(2,1)} %param.9) | copy-start | bytes 12582916
  441.2 7.4 copy-start.11
  455.4 97.2 %all-to-all-start.3 = ((bf16[128,16,1024]{2,1,0:T(8,128)(2,1)}), bf16[128,16,1024]{2,1,0:T(8,128)(2,1)}, u32[]{:S(2)}, u32[]{:S(2)}) async-start(bf16[128,16,1024]{2,1,0:T(8,128)(2,1)} %copy.78), calls=%async_computation.3 | async-start | bytes 8388608 | tf_op jit(solution)/shard_map/all_to_all | solution.py:41
  460.2 229.7 %all-reduce.4.cloned.1.call-start = ((), (), s32[]{:S(2)}) async-start(), calls=%async_computation.8 | async-start | bytes 2097152 | tf_op jit(solution)/shard_map/psum | solution.py:129
  470.2 17.0 %copy-start.10 = (bf16[256,8,8,128]{3,2,1,0:T(8,128)(2,1)S(1)}, bf16[256,8,8,128]{3,2,1,0:T(8,128)(2,1)}, u32[]{:S(2)}) copy-start(bf16[256,8,8,128]{3,2,1,0:T(8,128)(2,1)} %copy-done.9) | copy-start | bytes 12582916
  470.2 17.0 %copy-start.12 = (bf16[256,8,8,128]{3,2,1,0:T(8,128)(2,1)S(1)}, bf16[256,8,8,128]{3,2,1,0:T(8,128)(2,1)}, u32[]{:S(2)}) copy-start(bf16[256,8,8,128]{3,2,1,0:T(8,128)(2,1)} %copy-done.11) | copy-start | bytes 12582916
  552.6 6.0 copy-start.18
  561.4 289.7 %reduce-scatter.2.cloned.1.call-start = ((), (), s32[]{:S(2)}) async-start(), calls=%async_computation.7 | async-start | bytes 12976128 | tf_op jit(solution)/shard_map/reduce_scatter | solution.py:96
  572.3 12.1 %copy-start.6 = (bf16[256,8,8,128]{3,2,1,0:T(8,128)(2,1)S(1)}, bf16[256,8,8,128]{3,2,1,0:T(8,128)(2,1)}, u32[]{:S(2)}) copy-start(bf16[256,8,8,128]{3,2,1,0:T(8,128)(2,1)} %copy-done.5) | copy-start | bytes 12582916
  572.3 12.1 %copy-start.16 = (bf16[8,128,128]{2,1,0:T(8,128)(2,1)S(1)}, bf16[8,128,128]{2,1,0:T(8,128)(2,1)}, u32[]{:S(2)}) copy-start(bf16[8,128,128]{2,1,0:T(8,128)(2,1)} %param.12) | copy-start | bytes 786436
  589.1 9.3 %copy-start.21 = (f32[2048]{0:T(1024)S(1)}, f32[2048]{0:T(1024)}, u32[]{:S(2)}) copy-start(f32[2048]{0:T(1024)} %copy-done.20) | copy-start | bytes 24580
  647.6 206.8 %copy-start.1 = (bf16[8,128,128]{2,1,0:T(8,128)(2,1)S(1)}, bf16[8,128,128]{2,1,0:T(8,128)(2,1)}, u32[]{:S(2)}) copy-start(bf16[8,128,128]{2,1,0:T(8,128)(2,1)} %param.13) | copy-start | bytes 786436
  (8 other events, 24.4 us)
Sparse Core Ops, SparseCore 0:
  39.0 113.3 all-gather.4
  161.2 120.1 all-gather.2
  561.6 128.2 all-reduce.3
  696.8 154.3 reduce-scatter.1
where the time goes:
time: 867 us; the launch traced here: 861 us
  waiting for transfers between devices  446 us (51%)
  blocking collectives  135 us (16%)
  matrix products  108 us (12%)
  other arithmetic  76.8 us (9%)
  local copies, waits for them, and re-layouts  63.3 us (7%)
  starting transfers between devices  17.5 us (2%)
  between operations  14.6 us (2%)
    reduce_scatter x1, waiting for transfers between devices, on_device(): lax.psum_scatter(jnp.concatenate([gate_up_part, down_part], axis=1), ('dp...  159 us
    all_to_all x2, waiting for transfers between devices, into_fine(): lax.all_to_all(block_data, 'seq', split_axis=0, concat_axis=1, tiled=True)  147 us
    all_to_all x1, blocking collectives, into_coarse(): lax.all_to_all(block_data, 'seq', split_axis=1, concat_axis=0, tiled=True)  97.4 us
    all_to_all x1, waiting for transfers between devices, into_coarse(): lax.all_to_all(block_data, 'seq', split_axis=1, concat_axis=0, tiled=True)  96.8 us
    psum x1, blocking collectives, on_device(): lax.psum((fine_term, coarse_term, gain_mix_term, gain_mlp_term), ('dp', '...  38.1 us
    psum x1, waiting for transfers between devices, on_device(): lax.psum((fine_term, coarse_term, gain_mix_term, gain_mlp_term), ('dp', '...  30.2 us
    dot_general x1, matrix products, on_device(): lax.dot_general(back_both, full_gate_up, (((1,), (1,)), ((), ())), prefer...  17.9 us
  transfers between devices with their start and end apart: 7, of which 6 were waited for; matrix products, arithmetic and copies ran while one was open for 16% of the time, Pallas kernels for 0%

commit v1 on v0

v1 whole, which is shorter than its diff:
```python
import functools
import math

import jax
import jax.numpy as jnp
from jax import lax
from jax.experimental import pallas as pl
from jax.experimental.pallas import tpu as pltpu
from jax.sharding import PartitionSpec as P

D = 1024
FF = 1024
NB = 128
NC = 128
GW = 128
G = D // GW
HG = G // 2
HALF = D // 2
STRIP = 256

epsilon = 1e-05
F32 = jnp.float32
BF16 = jnp.bfloat16
NT = (((1,), (1,)), ((), ()))
MIB = 1 << 20


def dot(left, right):
    return jnp.dot(left, right, preferred_element_type=F32)


def dot_nt(left, right):
    return lax.dot_general(left, right, NT, preferred_element_type=F32)


def inv_rms(values):
    return lax.rsqrt(jnp.mean(values * values, axis=-1, keepdims=True) + epsilon)


def params(mib):
    return pltpu.CompilerParams(vmem_limit_bytes=mib * MIB)


def cost():
    return pl.CostEstimate(flops=1, bytes_accessed=1, transcendentals=0)


class Order:
    before = []

    @classmethod
    def mark(cls, *values):
        cls.before = list(values)

    @classmethod
    def also(cls, *values):
        cls.before = cls.before + list(values)


def run(kernel, in_specs, operands, **rest):
    extra = Order.before
    count = len(operands)

    def body(*refs):
        kernel(*refs[:count], *refs[count + len(extra):])

    outs = pl.pallas_call(
        body,
        in_specs=list(in_specs) + [pl.BlockSpec(memory_space=pl.ANY)] * len(extra),
        cost_estimate=cost(),
        **rest,
    )(*operands, *extra)
    Order.mark(outs[-1] if isinstance(outs, (list, tuple)) else outs)
    return outs


def lanes_of(blocks, group):
    part = slice(group * GW, (group + 1) * GW)
    return jnp.concatenate([blocks[i, :, part] for i in range(blocks.shape[0])], axis=1)


def spread(rows, plane, own, other, count, width):
    for slot, out in enumerate((own, other)):
        half = plane if slot == 0 else 1 - plane
        for local in range(HG):
            for b in range(width):
                at = (local * width + b) * GW
                took = rows[half * HG + local, pl.ds(b, count, stride=width), :]
                out[:, at:at + GW] = took.astype(BF16)


def collect(rows, plane, own, other, count, width):
    for slot, part in enumerate((own, other)):
        half = plane if slot == 0 else 1 - plane
        for local in range(HG):
            for b in range(width):
                at = (local * width + b) * GW
                took = part[:, at:at + GW].astype(F32)
                rows[half * HG + local, pl.ds(b, count, stride=width), :] = took
    return jnp.concatenate([rows[group] for group in range(G)], axis=1)


def fine_kernel(unit, starts, plane, tok, gain, factor, *refs):
    outs, hidden, rows = refs[:-2], refs[-2], refs[-1]
    count = tok.shape[0]
    low = min(starts)
    span = rows.shape[0] // count
    high = low + span
    for i in range(count):
        source = tok[i].astype(F32)
        hidden[i] = (source * inv_rms(source) * gain[...]).astype(BF16)
    for slot in range(2):
        half = plane[0] if slot == 0 else 1 - plane[0]
        for local in range(HG):
            group = half * HG + local
            lanes = pl.ds(pl.multiple_of(group * GW, GW), GW)
            side = jnp.concatenate([hidden[i, :, lanes] for i in range(count)], axis=1)
            mixed = dot(factor[group, low:high], side)
            for i in range(count):
                rows[i * span:(i + 1) * span, :] = mixed[:, i * GW:(i + 1) * GW]
            for chunk, start in enumerate(starts):
                out = outs[chunk] if slot == 0 else outs[-1]
                units = outs[chunk].shape[1] // (HG * unit * GW)
                skip = chunk * units if slot == 1 else 0
                start -= low
                for u in range(units):
                    for b in range(unit):
                        at = (((skip + u) * HG + local) * unit + b) * GW
                        took = rows[pl.ds(start + u * unit + b, count, stride=span), :]
                        out[:, at:at + GW] = took.astype(BF16)


def fine_forward(plane, tokens, gain, factor, starts, widths, unit):
    blocks = tokens.shape[0]
    shapes = [(blocks, width * HALF) for width in widths]
    shapes.append((blocks, sum(widths) * HALF))
    full = lambda shape: pl.BlockSpec(shape, lambda i: (0,) * len(shape))
    return run(
        functools.partial(fine_kernel, unit, starts),
        grid=(1,),
        in_specs=[
            pl.BlockSpec(memory_space=pltpu.SMEM),
            full((blocks, NB, D)),
            full((1, D)),
            full((G, NB, NB)),
        ],
        out_specs=[full(shape) for shape in shapes],
        out_shape=[jax.ShapeDtypeStruct(shape, BF16) for shape in shapes],
        scratch_shapes=[pltpu.VMEM((blocks, NB, D), BF16), pltpu.VMEM((blocks * sum(widths), GW), F32)],
        compiler_params=params(48),
        operands=[plane, tokens, gain, factor],
        name="fine_forward",
    )


def join_kernel(plane, own, other, out, rows):
    count, width = out.shape[:2]
    out[...] = collect(rows, plane[0], own, other, count, width).astype(BF16).reshape(out.shape)


def join(plane, own, other, unit):
    blocks, lanes = own.shape
    width = lanes // HALF
    half = pl.BlockSpec((blocks, unit * HALF), lambda i: (0, i))
    return run(
        join_kernel,
        grid=(width // unit,),
        in_specs=[pl.BlockSpec(memory_space=pltpu.SMEM), half, half],
        out_specs=pl.BlockSpec((blocks, unit, D), lambda i: (0, i, 0)),
        out_shape=jax.ShapeDtypeStruct((blocks, width, D), BF16),
        scratch_shapes=[pltpu.VMEM((G, blocks * unit, GW), F32)],
        compiler_params=params(24),
        operands=[plane, own, other],
        name="join",
    )


def coarse_kernel(count, *refs):
    weight, base, part = refs[count:]
    stacked = jnp.concatenate([raw[...] for raw in refs[:count]], axis=0)
    high = base.shape[0]
    lanes = base.shape[1] // HG
    for group in range(HG):
        strip = slice(group * lanes, (group + 1) * lanes)
        total = dot(weight[group], stacked[:, strip]).astype(BF16)
        base[:, strip] = total[:high]
        part[:, strip] = total[high:]


def coarse_mix(raws, weight, unit):
    lanes = raws[0].shape[1]
    tile = unit * HALF
    out_rows = weight.shape[1] // 2
    half = pl.BlockSpec((out_rows, tile), lambda t: (0, t))
    return run(
        functools.partial(coarse_kernel, len(raws)),
        grid=(lanes // tile,),
        in_specs=[
            *[pl.BlockSpec((raw.shape[0], tile), lambda t: (0, t)) for raw in raws],
            pl.BlockSpec(weight.shape, lambda t: (0, 0, 0)),
        ],
        out_specs=[half, half],
        out_shape=[jax.ShapeDtypeStruct((out_rows, lanes), BF16)] * 2,
        compiler_params=params(32),
        operands=[*raws, weight],
        name="coarse_mix",
    )


def stack_kernel(own, other, out):
    count = own.shape[0]
    out[:count] = own[...]
    out[count:] = other[...]


def stack(own, other, unit, at=0):
    blocks, lanes = own.shape
    tile = unit * HALF
    skip = at * lanes // tile
    half = pl.BlockSpec((blocks, tile), lambda t: (0, t))
    taken = pl.BlockSpec((blocks, tile), lambda t: (0, skip + t))
    return run(
        stack_kernel,
        grid=(lanes // tile,),
        in_specs=[half, taken],
        out_specs=pl.BlockSpec((2 * blocks, tile), lambda t: (0, t)),
        out_shape=jax.ShapeDtypeStruct((2 * blocks, lanes), BF16),
        compiler_params=params(16),
        operands=[own, other],
        name="stack",
    )


def add_kernel(flag, base, extra, own, other):
    count = own.shape[0]
    more = jnp.where(flag[0] == 1, extra[...].astype(F32), 0.0)
    total = (base[...].astype(F32) + more).astype(BF16)
    own[...] = total[:count]
    other[...] = total[count:]


def add_split(flag, base, extra, unit):
    blocks, lanes = base.shape[0] // 2, base.shape[1]
    tile = unit * HALF
    whole = pl.BlockSpec((2 * blocks, tile), lambda t: (0, t))
    half = pl.BlockSpec((blocks, tile), lambda t: (0, t))
    return run(
        add_kernel,
        grid=(lanes // tile,),
        in_specs=[pl.BlockSpec(memory_space=pltpu.SMEM), whole, whole],
        out_specs=[half, half],
        out_shape=[jax.ShapeDtypeStruct((blocks, lanes), BF16)] * 2,
        compiler_params=params(16),
        operands=[flag, base, extra],
        name="add_split",
    )


def coarse_grad_kernel(ups, downs, *refs):
    upper = jnp.concatenate([ref[...] for ref in refs[:ups]], axis=0)
    lower = jnp.concatenate([ref[...] for ref in refs[ups:ups + downs]], axis=0)
    out = refs[-1]
    lanes = upper.shape[1] // HG

    @pl.when(pl.program_id(0) == 0)
    def _():
        out[...] = jnp.zeros_like(out)

    for group in range(HG):
        strip = slice(group * lanes, (group + 1) * lanes)
        out[group] += dot_nt(upper[:, strip], lower[:, strip])


def coarse_grad(uppers, lowers, unit):
    lanes = uppers[0].shape[1]
    tile = unit * HALF
    high = sum(u.shape[0] for u in uppers)
    wide = sum(v.shape[0] for v in lowers)
    return run(
        functools.partial(coarse_grad_kernel, len(uppers), len(lowers)),
        grid=(lanes // tile,),
        in_specs=[pl.BlockSpec((v.shape[0], tile), lambda t: (0, t)) for v in uppers + lowers],
        out_specs=pl.BlockSpec((HG, high, wide), lambda t: (0, 0, 0)),
        out_shape=jax.ShapeDtypeStruct((HG, high, wide), F32),
        compiler_params=params(32),
        operands=[*uppers, *lowers],
        name="coarse_grad",
    )


def mlp_kernel(plane, tok, cot, own, other, gain_mix, gain_mlp, weights, *refs):
    layer, mlp_in, active, back_both, back_after, mixed, back_own, back_other = refs[-10:-2]
    gain_sum, rows = refs[-2:]
    shape = tok.shape
    flat = (shape[0] * shape[1], D)
    taken = collect(rows, plane[0], own, other, shape[0], shape[1])
    mixed[...] = taken.astype(BF16).reshape(shape)
    source = tok[...].reshape(flat).astype(F32)
    hidden = (source * inv_rms(source) * gain_mix[...]).astype(BF16).astype(F32)
    after = source + taken * hidden
    scale = inv_rms(after)
    normed = after * scale
    entering = (normed * gain_mlp[...]).astype(BF16)
    mlp_in[...] = entering.reshape(shape)
    upstream = cot[...].reshape(flat)
    active_parts, gate_parts, up_parts = [], [], []
    for start in range(0, FF, STRIP):
        strip = slice(start, start + STRIP)
        gate = dot(entering, weights[:, strip])
        upward = dot(entering, weights[:, FF + start:FF + start + STRIP])
        back_act = dot(upstream, weights[:, 2 * FF + start:2 * FF + start + STRIP])
        back_act = back_act.astype(BF16).astype(F32)
        squash = jax.nn.sigmoid(gate)
        silu = gate * squash
        slope = squash * (1.0 + gate * (1.0 - squash))
        active_parts.append((silu * upward).astype(BF16))
        gate_parts.append((back_act * upward * slope).astype(BF16))
        up_parts.append((back_act * silu).astype(BF16))
    activation = jnp.concatenate(active_parts, axis=1)
    back_gate = jnp.concatenate(gate_parts, axis=1)
    back_up = jnp.concatenate(up_parts, axis=1)
    active[...] = activation.reshape(shape)
    back_both[:, :, :FF] = back_gate.reshape(shape)
    back_both[:, :, FF:] = back_up.reshape(shape)
    layer[...] = (after + dot_nt(activation, weights[:, 2 * FF:])).astype(BF16).reshape(shape)
    back_in = dot_nt(back_gate, weights[:, :FF]) + dot_nt(back_up, weights[:, FF:2 * FF])

    @pl.when(pl.program_id(0) == 0)
    def _():
        gain_sum[...] = jnp.zeros_like(gain_sum)

    gain_sum[...] += jnp.sum(back_in * normed, axis=0, keepdims=True)
    weighted = back_in * gain_mlp[...]
    centre = jnp.mean(weighted * normed, axis=-1, keepdims=True)
    total = upstream.astype(F32) + scale * (weighted - normed * centre)
    back_after[...] = total.astype(BF16).reshape(shape)
    back_mixed = total * hidden
    for group in range(G):
        rows[group] = back_mixed[:, group * GW:(group + 1) * GW]
    spread(rows, plane[0], back_own, back_other, shape[0], shape[1])


def mlp(plane, tokens, cotangent, own, other, gain_mix, gain_mlp, weights, kept, start, unit):
    blocks, lanes = own.shape
    width = lanes // HALF
    first = start // unit
    whole = pl.BlockSpec((blocks, unit, D), lambda i: (0, first + i, 0))
    local = pl.BlockSpec((blocks, unit, D), lambda i: (0, i, 0))
    half = pl.BlockSpec((blocks, unit * HALF), lambda i: (0, i))
    gain = pl.BlockSpec((1, D), lambda i: (0, 0))
    operands = [plane, tokens, cotangent, own, other, gain_mix, gain_mlp, weights]
    specs = [pl.BlockSpec(memory_space=pltpu.SMEM), whole, whole, half, half, gain, gain]
    specs.append(pl.BlockSpec((D, 3 * FF), lambda i: (0, 0)))
    aliases = {len(operands) + i: i for i in range(len(kept))}
    operands += kept
    specs += [pl.BlockSpec(memory_space=pl.ANY)] * len(kept)
    part = jax.ShapeDtypeStruct((blocks, width, D), BF16)
    full = jax.ShapeDtypeStruct((blocks, NB, D), BF16)
    return run(
        mlp_kernel,
        grid=(width // unit,),
        in_specs=specs,
        out_specs=[
            whole,
            whole,
            whole,
            pl.BlockSpec((blocks, unit, 2 * FF), lambda i: (0, first + i, 0)),
            local,
            local,
            half,
            half,
            gain,
        ],
        out_shape=[
            full,
            full,
            full,
            jax.ShapeDtypeStruct((blocks, NB, 2 * FF), BF16),
            part,
            part,
            jax.ShapeDtypeStruct((blocks, lanes), BF16),
            jax.ShapeDtypeStruct((blocks, lanes), BF16),
            jax.ShapeDtypeStruct((1, D), F32),
        ],
        scratch_shapes=[pltpu.VMEM((G, blocks * unit, GW), F32)],
        input_output_aliases=aliases,
        compiler_params=params(56),
        operands=operands,
        name="mlp",
    )


def weight_kernel(has_prior, mlp_in, active, back_both, cot, *refs):
    outs, total = refs[-3:-1], refs[-1]
    count = mlp_in.shape[0] * mlp_in.shape[1]
    step, steps = pl.program_id(0), pl.num_programs(0)
    turn = (((0,), (0,)), ((), ()))
    entering = mlp_in[...].reshape(count, D)
    upstream = cot[...].reshape(count, D)

    @pl.when(step == 0)
    def _():
        total[...] = jnp.zeros_like(total)

    for start in range(0, 3 * FF, STRIP):
        if start < 2 * FF:
            left, right = entering, back_both[:, :, start:start + STRIP]
        else:
            left, right = upstream, active[:, :, start - 2 * FF:start - 2 * FF + STRIP]
        total[:, start:start + STRIP] += lax.dot_general(
            left, right.reshape(count, STRIP), turn, preferred_element_type=F32
        )

    @pl.when(step == steps - 1)
    def _():
        for i, out in enumerate(outs):
            wide = out.shape[1]
            result = total[:, i * wide:(i + 1) * wide]
            if has_prior:
                result = result + refs[i][...].astype(F32)
            out[...] = result.astype(BF16)


def weight_grads_of(kept, cotangent, prior, low, high, unit):
    blocks = cotangent.shape[0]
    first = low // unit
    block = pl.BlockSpec((blocks, unit, D), lambda k: (0, first + k, 0))
    wide = pl.BlockSpec((blocks, unit, 2 * FF), lambda k: (0, first + k, 0))
    half = pl.BlockSpec((D, 3 * FF // 2), lambda k: (0, 0))
    return run(
        functools.partial(weight_kernel, bool(prior)),
        grid=((high - low) // unit,),
        in_specs=[block, block, wide, block] + [half] * len(prior),
        out_specs=[half, half],
        out_shape=[jax.ShapeDtypeStruct((D, 3 * FF // 2), BF16)] * 2,
        scratch_shapes=[pltpu.VMEM((D, 3 * FF), F32)],
        compiler_params=params(56),
        operands=[kept[1], kept[2], kept[3], cotangent, *prior],
        name="weight_grad",
    )


def finish(source, gain, back_after, mixed, blocked):
    scale = inv_rms(source)
    normed = source * scale
    back_hidden = back_after * mixed + blocked
    weighted = back_hidden * gain
    centre = jnp.mean(weighted * normed, axis=-1, keepdims=True)
    return back_hidden * normed, back_after + scale * (weighted - normed * centre)


def tail_kernel(count, unit, tok, gain, factor, *refs):
    backs, mixes, fines = (refs[i * count:(i + 1) * count] for i in range(3))
    grad, rest, fine_term, gain_sum, blocked = refs[3 * count:]
    steps = tok.shape[0]

    @pl.when(pl.program_id(0) == 0)
    def _():
        fine_term[...] = jnp.zeros_like(fine_term)
        gain_sum[...] = jnp.zeros_like(gain_sum)

    source = tok[...].astype(F32)
    hidden = (source * inv_rms(source) * gain[...]).astype(BF16)
    back_fine = jnp.concatenate([ref[...] for ref in fines], axis=1)
    for group in range(G):
        upper = lanes_of(back_fine, group)
        result = dot(factor[group], upper)
        for i in range(steps):
            blocked[i, :, group * GW:(group + 1) * GW] = result[:, i * GW:(i + 1) * GW]
        fine_term[group] += dot_nt(upper, lanes_of(hidden, group))
    back_after = jnp.concatenate([ref[...] for ref in backs], axis=1).astype(F32)
    mixed = jnp.concatenate([ref[...] for ref in mixes], axis=1).astype(F32)
    terms, grads = finish(source[:, unit:], gain[...], back_after, mixed, blocked[:, unit:])
    gain_sum[...] += jnp.sum(jnp.sum(terms, axis=0), axis=0, keepdims=True)
    grad[:, unit:] = grads.astype(BF16)
    grad[:, :unit] = jnp.zeros_like(grad[:, :unit])
    rest[...] = blocked[:, :unit]


def tail(tokens, gain, factor, backs, mixes, fines, unit):
    blocks = tokens.shape[0]
    step = min(2, blocks)
    one = pl.BlockSpec((step, NB, D), lambda i: (i, 0, 0))

    def rows(arrays):
        return [pl.BlockSpec((step, v.shape[1], D), lambda i: (i, 0, 0)) for v in arrays]

    return run(
        functools.partial(tail_kernel, len(backs), unit),
        grid=(blocks // step,),
        in_specs=[
            one,
            pl.BlockSpec((1, D), lambda i: (0, 0)),
            pl.BlockSpec(factor.shape, lambda i: (0, 0, 0)),
            *rows(backs),
            *rows(mixes),
            *rows(fines),
        ],
        out_specs=[
            one,
            pl.BlockSpec((step, unit, D), lambda i: (i, 0, 0)),
            pl.BlockSpec((G, NB - unit, NB), lambda i: (0, 0, 0)),
            pl.BlockSpec((1, D), lambda i: (0, 0)),
        ],
        out_shape=[
            jax.ShapeDtypeStruct((blocks, NB, D), BF16),
            jax.ShapeDtypeStruct((blocks, unit, D), F32),
            jax.ShapeDtypeStruct((G, NB - unit, NB), F32),
            jax.ShapeDtypeStruct((1, D), F32),
        ],
        scratch_shapes=[pltpu.VMEM((step, NB, D), F32)],
        compiler_params=params(48),
        operands=[tokens, gain, factor, *backs, *mixes, *fines],
        name="fine_backward",
    )


def last_kernel(tok, gain, factor, back, mix, fine, rest, _, grad, fine_term, gain_sum, blocked):
    blocks = tok.shape[0]
    source = tok[...].astype(F32)
    hidden = (source * inv_rms(source) * gain[...]).astype(BF16)
    back_fine = fine[...]
    for group in range(G):
        upper = lanes_of(back_fine, group)
        result = dot(factor[group], upper)
        for i in range(blocks):
            part = slice(group * GW, (group + 1) * GW)
            blocked[i, :, part] = rest[i, :, part] + result[:, i * GW:(i + 1) * GW]
        fine_term[group] = dot_nt(upper, lanes_of(hidden, group))
    terms, grads = finish(source, gain[...], back[...].astype(F32), mix[...].astype(F32), blocked[...])
    gain_sum[...] = jnp.sum(jnp.sum(terms, axis=0), axis=0, keepdims=True)
    grad[...] = grads.astype(BF16)


def last(tokens, gain, factor, back, mix, fine, rest, grad):
    blocks, unit = back.shape[:2]
    one = pl.BlockSpec((blocks, unit, D), lambda i: (0, 0, 0))
    return run(
        last_kernel,
        grid=(1,),
        in_specs=[
            one,
            pl.BlockSpec((1, D), lambda i: (0, 0)),
            pl.BlockSpec(factor.shape, lambda i: (0, 0, 0)),
            one,
            one,
            one,
            one,
            pl.BlockSpec(memory_space=pl.ANY),
        ],
        out_specs=[
            one,
            pl.BlockSpec((G, unit, unit), lambda i: (0, 0, 0)),
            pl.BlockSpec((1, D), lambda i: (0, 0)),
        ],
        out_shape=[
            jax.ShapeDtypeStruct(grad.shape, BF16),
            jax.ShapeDtypeStruct((G, unit, unit), F32),
            jax.ShapeDtypeStruct((1, D), F32),
        ],
        input_output_aliases={7: 0},
        scratch_shapes=[pltpu.VMEM((blocks, unit, D), F32)],
        compiler_params=params(48),
        operands=[tokens, gain, factor, back, mix, fine, rest, grad],
        name="fine_backward_last",
    )


def reduce_all(value, axes, first=1):
    for axis in axes:
        size = lax.axis_size(axis)
        reach = first
        while reach < size:
            pairs = [(i, i ^ reach) for i in range(size)]
            value = value + lax.ppermute(value, axis, pairs)
            reach *= 2
    return value


def split_kernel(inner, has_arrived, bit, value, *refs):
    keep, away = refs[-2:]
    side = bit[0]
    for j in range(keep.shape[0]):
        base = j // inner * 2 * inner + j % inner
        mine, theirs = base + side * inner, base + (1 - side) * inner
        if has_arrived:
            keep[j] = value[mine] + refs[0][mine]
            away[j] = value[theirs] + refs[0][theirs]
        else:
            keep[j] = value[mine]
            away[j] = value[theirs]


def split(bit, value, arrived, inner):
    shape = (value.shape[0] // 2,) + value.shape[1:]
    full = lambda shape: pl.BlockSpec(shape, lambda i: (0,) * len(shape))
    more = [] if arrived is None else [arrived]
    return run(
        functools.partial(split_kernel, inner, bool(more)),
        grid=(1,),
        in_specs=[pl.BlockSpec(memory_space=pltpu.SMEM)] + [full(value.shape)] * (1 + len(more)),
        out_specs=[full(shape)] * 2,
        out_shape=[jax.ShapeDtypeStruct(shape, BF16)] * 2,
        compiler_params=params(32),
        operands=[bit, value, *more],
        name="split",
    )


class Scatter:

    def __init__(self, value, late):
        bits = []
        for axis in ("dp", "seq"):
            size = lax.axis_size(axis)
            bits += [(axis, 1 << k) for k in reversed(range(size.bit_length() - 1))]
        outer = [bit for bit in reversed(bits) if bit[0] == "dp"]
        inner = [bit for bit in reversed(bits) if bit[0] == "seq"]
        self.order = outer[:1] + inner[:1] + outer[1:] + inner[1:] if late else outer + inner
        self.left = bits
        self.columns = value.shape[1]
        self.value = value.reshape(2 ** len(bits), -1, self.columns)
        self.arriving = None

    def step(self):
        if not self.order:
            self.value, self.arriving = self.value + self.arriving, None
            return
        axis, reach = self.order.pop(0)
        at = self.left.index((axis, reach))
        self.left = self.left[:at] + self.left[at + 1:]
        inner = 2 ** (len(self.left) - at)
        size = lax.axis_size(axis)
        bit = ((lax.axis_index(axis) // reach) % 2).astype(jnp.int32).reshape(1)
        self.value, away = split(bit, self.value, self.arriving, inner)
        self.arriving = lax.ppermute(away, axis, [(i, i ^ reach) for i in range(size)])


def gather_rows(value):
    steps = []
    for axis in ("seq", "dp"):
        size = lax.axis_size(axis)
        reaches = [1 << k for k in range(size.bit_length() - 1)]
        steps += [(axis, reach) for reach in reversed(reaches)]
    rows, columns = value.shape
    value = value[None]
    for axis, reach in steps:
        pairs = [(i, i ^ reach) for i in range(lax.axis_size(axis))]
        other = lax.ppermute(value, axis, pairs)
        low = lax.axis_index(axis) // reach % 2 == 0
        value = jnp.concatenate(
            [jnp.where(low, value, other), jnp.where(low, other, value)], axis=0
        )
    count = len(steps)
    stepped = list(reversed(steps))
    wanted = [(axis, 1 << k) for axis in ("dp", "seq")
              for k in reversed(range(lax.axis_size(axis).bit_length() - 1))]
    value = value.reshape((2,) * count + (rows, columns))
    order = [stepped.index(bit) for bit in wanted]
    return value.transpose(*order, count, count + 1).reshape(-1, columns)


def on_device(tokens, cotangent, gain_mix, gain_mlp, fine_factor, coarse_factor, w_gate_up, w_down):
    rows = tokens.shape[1]
    blocks = rows // NB
    seq_devices = lax.axis_size("seq")
    data_devices = lax.axis_size("dp")
    planes = 2
    depth = seq_devices // planes
    index = lax.axis_index("seq")
    level, plane = index // planes, index % planes
    unit = max(16, 256 // blocks)
    width = min(2 * unit, NB // 2)
    widths = [width] * (NB // width)

    def shift(value, by, low=0, high=None):
        top = depth - 1 if high is None else high
        pairs = [
            (lv * planes + p, (lv + by) * planes + p)
            for lv in range(depth)
            for p in range(planes)
            if low <= lv + by <= top
        ]
        return lax.ppermute(value, "seq", pairs)

    def swap(value):
        return lax.ppermute(value, "seq", [(i, i ^ 1) for i in range(seq_devices)])

    weights = gather_rows(jnp.concatenate([w_gate_up, w_down], axis=1))
    token_blocks = tokens.reshape(blocks, NB, D)
    cot_blocks = cotangent.reshape(blocks, NB, D)
    row_mix, row_mlp = gain_mix.reshape(1, D), gain_mlp.reshape(1, D)

    pair = planes * blocks
    local = jnp.arange(pair)
    order = jnp.where(plane == 0, local, (local + blocks) % pair)

    def picks(*levels):
        wanted = jnp.concatenate([order + lv * pair for lv in levels])
        return (wanted[:, None] == jnp.arange(NC)[None, :]).astype(BF16)

    reaches = list(range(max(2, depth - 1)))
    far = reaches[-1]
    up_levels = [level - d for d in reaches[:-1]] + [jnp.where(level == far, 0, depth)]
    down_levels = [level + d for d in reaches[:-1]] + [jnp.where(level == 1, depth - 1, depth)]
    rows_up, columns_up = picks(level, level + 1), picks(*up_levels)
    rows_down, columns_down = picks(level, level - 1), picks(*down_levels)
    spot = (jnp.arange(2 * pair)[:, None] >= pair) & (jnp.arange(len(reaches) * pair)[None] < pair)
    factor = lax.dynamic_slice_in_dim(coarse_factor, plane * HG, HG, axis=0)

    def chosen(matrix, rows_of, columns_of):
        some = jnp.einsum("rp,gpq->grq", rows_of, matrix, preferred_element_type=F32)
        some = jnp.einsum(
            "grq,cq->grc", some.astype(BF16), columns_of, preferred_element_type=F32
        )
        return jnp.where(spot, 0.0, some).astype(BF16)

    which = plane.reshape(1).astype(jnp.int32)
    count = len(widths)
    starts = [NB - sum(widths[:i + 1]) for i in range(count)]
    steps = range(count)
    state = [dict() for _ in steps]
    kept = []
    sums = {}
    Order.mark()

    def forward(*chunks):
        outs = fine_forward(
            which, token_blocks, row_mix, fine_factor,
            [starts[c] for c in chunks], [widths[c] for c in chunks], unit,
        )
        arrived = swap(outs[-1])
        for at, c in enumerate(chunks):
            state[c]["pair"] = outs[at], arrived, at

    last_flag = (level == depth - 1).astype(jnp.int32).reshape(1)
    first_flag = (level == 0).astype(jnp.int32).reshape(1)

    def jump_up(here, part):
        pairs = []
        for p in range(planes):
            if here is not None:
                pairs.append((p, far * planes + p))
            if part is not None:
                pairs.append((far * planes + p, (depth - 1) * planes + p))
        both = here if part is None else part if here is None else jnp.where(level == 0, here, part)
        return lax.ppermute(both, "seq", pairs)

    def jump_down(here, part):
        pairs = []
        for p in range(planes):
            if here is not None:
                pairs.append(((depth - 1) * planes + p, planes + p))
            if part is not None:
                pairs.append((planes + p, p))
        both = here if part is None else part if here is None else jnp.where(level == 1, part, here)
        return lax.ppermute(both, "seq", pairs)

    def stack_up(c):
        here = part = None
        if c > 0:
            part = state[c - 1]["part"]
        if c < count:
            here = stack(*state[c]["pair"][:2], unit, state[c]["pair"][2])
            middle = [shift(here, d, high=depth - 2) for d in reaches[2:-1]]
            raws = [here, shift(here, 1)] + middle
        leap = jump_up(here, part)
        if c > 0:
            state[c - 1]["extra"] = leap
        if c < count:
            state[c]["raws"] = raws + [leap]

    def mix_up(c):
        state[c]["base"], state[c]["part"] = coarse_mix(state[c]["raws"], up_weight, unit)

    def add_up(c):
        own, other = add_split(last_flag, state[c]["base"], state[c]["extra"], unit)
        state[c]["own"], state[c]["other"] = own, swap(other)

    def run_mlp(c, kept):
        outs = mlp(
            which, token_blocks, cot_blocks, state[c]["own"], state[c]["other"], row_mix, row_mlp,
            weights, kept, starts[c], unit,
        )
        names = ["back_after", "mixed", "down_own", "down_other"]
        state[c].update(zip(names, outs[4:8]))
        sums["gain"] = outs[8] if c == 0 else sums["gain"] + outs[8]
        state[c]["down_other"] = swap(state[c]["down_other"])
        return list(outs[:4])

    def weight_grad(first, end):
        sums["weights"] = weight_grads_of(
            kept, cot_blocks, sums.get("weights", []), starts[end - 1],
            starts[first] + widths[first], unit,
        )

    def stack_down(c):
        here = part = None
        if c > 0:
            part = state[c - 1]["part"]
        if c < count:
            here = stack(state[c]["down_own"], state[c]["down_other"], unit)
            middle = [shift(here, -d, low=1) for d in reaches[2:-1]]
            backs = [here, shift(here, -1)] + middle
        leap = jump_down(here, part)
        if c > 0:
            state[c - 1]["extra"] = leap
        if c < count:
            state[c]["backs"] = backs + [leap]

    def mix_down(c):
        state[c]["base"], state[c]["part"] = coarse_mix(state[c]["backs"], down_weight, unit)

    def add_down(c):
        own, other = add_split(first_flag, state[c]["base"], state[c]["extra"], unit)
        state[c]["fine_own"], state[c]["fine_other"] = own, swap(other)

    def factor_grad(c):
        part = coarse_grad(state[c]["backs"][:2], state[c]["raws"], unit)
        sums["coarse"] = part if c == 0 else sums["coarse"] + part

    def join_down(c):
        state[c]["fine"] = join(which, state[c]["fine_own"], state[c]["fine_other"], unit)

    def scatter_step():
        for part in scatters:
            part.step()

    halfway = count - 1
    up_weight = chosen(factor, rows_up, columns_up)
    down_weight = chosen(factor.transpose(0, 2, 1), rows_down, columns_down)
    forward(0)
    stack_up(0)
    forward(*steps[1:])
    for i in range(count + 1):
        if i < count:
            mix_up(i)
            stack_up(i + 1)
        if i >= 4:
            join_down(i - 4)
        if i >= 1:
            add_up(i - 1)
            if i == count:
                weight_grad(0, halfway)
            kept = run_mlp(i - 1, kept)
        if i >= 2:
            mix_down(i - 2)
        if i >= 1:
            stack_down(i - 1)
        if i == count:
            weight_grad(halfway, count)
            scatters = [Scatter(value, late) for value, late in zip(sums["weights"], (False, True))]
            scatter_step()
        if i >= 2:
            factor_grad(i - 2)
        if i >= 3:
            add_down(i - 3)
    if count >= 3:
        join_down(count - 3)
    scatter_step()
    if count >= 2:
        add_down(count - 2)
    mix_down(count - 1)
    stack_down(count)
    factor_grad(count - 1)
    scatter_step()
    if count >= 2:
        join_down(count - 2)

    backs = [state[c]["back_after"] for c in reversed(steps)]
    mixes = [state[c]["mixed"] for c in reversed(steps)]
    fines = [None] + [state[c]["fine"] for c in reversed(steps[:-1])]
    gain_mlp_sum = sums["gain"]

    flipped = fine_factor.transpose(0, 2, 1)
    grad_in, rest, fine_high, gain_high = tail(
        token_blocks, row_mix, flipped[:, :, width:], backs[1:], mixes[1:], fines[1:], width
    )
    coarse_sum = sums["coarse"]
    valid = (jnp.arange(2 * pair) < pair)[:, None] | (level == depth - 2)
    part = jnp.where(valid & ~spot, coarse_sum, 0.0).astype(BF16)
    part = jnp.einsum("rp,grc->gpc", rows_up, part, preferred_element_type=F32).astype(BF16)
    placed = jnp.einsum("gpc,cq->gpq", part, columns_up, preferred_element_type=F32).astype(BF16)
    cut = HG * NC
    joint = jnp.concatenate([placed.reshape(cut, NC), fine_high.astype(BF16).reshape(-1, NB)])
    joint = reduce_all(joint, ("dp",))
    Order.also(joint)
    add_down(count - 1)
    scatter_step()
    joint = reduce_all(joint, ("seq",), first=planes)
    join_down(count - 1)
    fines[0] = state[count - 1]["fine"]
    grad_in, fine_low, gain_low = last(
        token_blocks, row_mix, flipped[:, :width, :width], backs[0], mixes[0], fines[0], rest, grad_in
    )

    facing = swap(joint)
    coarse_all = jnp.where(
        plane == 0,
        jnp.concatenate([joint[:cut], facing[:cut]]),
        jnp.concatenate([facing[:cut], joint[:cut]]),
    ).astype(F32).reshape(G, NC, NC)
    fine_all = (joint[cut:].astype(F32) + facing[cut:].astype(F32)).reshape(G, -1, NB)
    small = jnp.concatenate(
        [
            fine_low.reshape(-1, D),
            gain_high + gain_low,
            gain_mlp_sum,
        ],
        axis=0,
    )
    small = reduce_all(small, ("dp", "seq"))
    while scatters[0].order or scatters[0].arriving is not None:
        scatter_step()
    weight_grads = jnp.concatenate(
        [part.value.reshape(-1, part.columns) for part in scatters], axis=1
    ).astype(F32)
    low_rows = small[:-2].reshape(G, width, width)
    low_rows = jnp.pad(low_rows, ((0, 0), (0, 0), (0, NB - width)))

    all_seqs = data_devices * tokens.shape[0]
    scale_tokens = 1.0 / math.sqrt(all_seqs * NC * NB)
    grad_fine = jnp.tril(jnp.concatenate([low_rows, fine_all], axis=1))
    grad_fine = grad_fine * (1.0 / math.sqrt(all_seqs * NC * GW))
    grad_coarse = jnp.tril(coarse_all) * (1.0 / math.sqrt(all_seqs * NB * GW))
    return (
        kept[0].reshape(1, rows, D),
        grad_in.reshape(1, rows, D),
        weight_grads[:, :2 * FF] * scale_tokens,
        weight_grads[:, 2 * FF:] * scale_tokens,
        grad_fine,
        grad_coarse,
        small[-2] * scale_tokens,
        small[-1] * scale_tokens,
    )


def solution(mesh):
    placed = (
        P("dp", "seq", None),
        P("dp", "seq", None),
        P(),
        P(),
        P(),
        P(),
        P(("dp", "seq"), None),
        P(("dp", "seq"), None),
    )
    return jax.shard_map(
        on_device,
        mesh=mesh,
        in_specs=placed,
        out_specs=(
            P("dp", "seq", None),
            P("dp", "seq", None),
            P(("dp", "seq"), None),
            P(("dp", "seq"), None),
            P(),
            P(),
            P(),
            P(),
        ),
        check_vma=False,
    )
```

time: 867 us -> 579 us (0.67)
  waiting for transfers between devices: 446 us -> 250 us
  Pallas kernels: 0 us -> 172 us
  blocking collectives: 135 us -> 0 us
  matrix products: 108 us -> 1.11 us
  starting transfers between devices: 17.5 us -> 78.6 us
  other arithmetic: 76.8 us -> 18.2 us
  local copies, waits for them, and re-layouts: 63.3 us -> 49.2 us
  between operations: 14.6 us -> 2.94 us
    ppermute x0 -> x57, waiting for transfers between devices: none -> 250 us  [the longest x8 69.9 us: shift(): return lax.ppermute(value, 'seq', pairs)]
    all_to_all x3 -> x0, waiting for transfers between devices: 244 us -> none  [the longest x2 147 us: into_fine(): lax.all_to_all(block_data, 'seq', split_axis=0, concat_axis=1, tiled=True)]
    pallas_call x0 -> x52, Pallas kernels: none -> 172 us  [run(): pl.pallas_call(body, in_specs=list(in_specs) + [pl.BlockSpec(memory_space...]
    reduce_scatter x1 -> x0, waiting for transfers between devices: 159 us -> none  [on_device(): lax.psum_scatter(jnp.concatenate([gate_up_part, down_part], axis=1), ('dp...]
    dot_general x12 -> x3, matrix products: 108 us -> 1.11 us  [the longest x2 0.68 us: chosen(): jnp.einsum('grq,cq->grc', some.astype(BF16), columns_of, preferred_elemen...]
    all_to_all x1 -> x0, blocking collectives: 97.4 us -> none  [into_coarse(): lax.all_to_all(block_data, 'seq', split_axis=1, concat_axis=0, tiled=True)]
    ppermute x0 -> x57, starting transfers between devices: none -> 78.6 us  [the longest x5 19.5 us: jump_up(): return lax.ppermute(both, 'seq', pairs)]
    psum x1 -> x0, blocking collectives: 38.1 us -> none  [on_device(): lax.psum((fine_term, coarse_term, gain_mix_term, gain_mlp_term), ('dp', '...]
  transfers between devices with their start and end apart: 7 -> 57, of which waited for: 6 -> 27; matrix products, arithmetic and copies ran while one was open for 16% -> 4% of each run, Pallas kernels for 0% -> 24%
where the time goes in v1:
time: 579 us; the launch traced here: 572 us
  waiting for transfers between devices  250 us (43%)
  Pallas kernels  172 us (30%)
  starting transfers between devices  78.6 us (14%)
  local copies, waits for them, and re-layouts  49.2 us (8%)
  other arithmetic  18.2 us (3%)
    pallas_call x52, Pallas kernels, run(): pl.pallas_call(body, in_specs=list(in_specs) + [pl.BlockSpec(memory_space...  172 us
    ppermute x8, waiting for transfers between devices, shift(): return lax.ppermute(value, 'seq', pairs)  69.9 us
    ppermute x5, waiting for transfers between devices, jump_up(): return lax.ppermute(both, 'seq', pairs)  57.5 us
    ppermute x15, waiting for transfers between devices, swap(): return lax.ppermute(value, 'seq', [(i, i ^ 1) for i in range(seq_devices)])  42.8 us
    unnamed x239, local copies, waits for them, and re-layouts  41.8 us
    ppermute x10, waiting for transfers between devices, step(): lax.ppermute(away, axis, [(i, i ^ reach) for i in range(size)])  27 us
    ppermute x9, waiting for transfers between devices, reduce_all(): value = value + lax.ppermute(value, axis, pairs)  23 us
    ppermute x5, waiting for transfers between devices, jump_down(): return lax.ppermute(both, 'seq', pairs)  21.6 us
  transfers between devices with their start and end apart: 57, of which 27 were waited for; matrix products, arithmetic and copies ran while one was open for 4% of the time, Pallas kernels for 24%

profile of v1, /device:TPU:0, one launch (start us, length us, event | category | flops | bytes accessed | tf_op | source)
XLA Modules:
  0.0 572.4 jit_solution(1137934566759709730)
XLA Ops:
  17.6 8.7 %collective-permute-done.10 = bf16[2,32,3072]{2,1,0:T(8,128)(2,1)S(1)} collective-permute-done((bf16[2,32,3072]{2,1,0:T(8,128)(2,1)S(1)}, bf16[2,32,3072]{2,1,0:T(8,128)(2,1)S(1)}, u32[]{:S(2)}, u32[]{:S(2)}) %collective-permute-start.10) | collective-permute-done | bytes 393248 | tf_op jit(solution)/shard_map/ppermute | solution.py:649
  28.5 10.5 %fine_forward.3 = (bf16[16,16384]{1,0:T(8,128)(2,1)S(1)}, bf16[16,16384]{1,0:T(8,128)(2,1)S(1)}, bf16[16,16384]{1,0:T(8,128)(2,1)S(1)}, bf16[16,49152]{1,0:T(8,128)(2,1)}) custom-call(s32[1]{0:T(128)} %bitcast.refs_0_, bf16[16,128,1024]{2,1,0:T(8,128)(2,1)} %bitcast.70, f32[1,1024]{1,0:T(1,128)S(1)} %bitcast.85, bf16[8,128,128]{2,1,0:T(8,128)(2,1)S(1)} %copy-done.38, ...), custom_call_target="tpu_custom_call" | custom-call | flops 1 | bytes 1 | tf_op jit(solution)/shard_map/fine_forward/pallas_call | solution.py:67
  54.5 16.0 %collective-permute-done.2.refs_1_.refs_3_ = bf16[32,16384]{1,0:T(8,128)(2,1)S(1)} collective-permute-done((bf16[32,16384]{1,0:T(8,128)(2,1)S(1)}, bf16[32,16384]{1,0:T(8,128)(2,1)S(1)}, u32[]{:S(2)}, u32[]{:S(2)}) %collective-permute-start.2) | collective-permute-done | bytes 1048608 | tf_op jit(solution)/shard_map/ppermute | solution.py:684
  70.5 19.5 %collective-permute-done.3.refs_2_.refs_4_ = bf16[32,16384]{1,0:T(8,128)(2,1)S(1)} collective-permute-done((bf16[32,16384]{1,0:T(8,128)(2,1)S(1)}, bf16[32,16384]{1,0:T(8,128)(2,1)S(1)}, u32[]{:S(2)}, u32[]{:S(2)}) %collective-permute-start.3) | collective-permute-done | bytes 1048608 | tf_op jit(solution)/shard_map/ppermute | solution.py:747
  100.2 38.0 %collective-permute-done.5.refs_2_.refs_4_ = bf16[32,16384]{1,0:T(8,128)(2,1)S(1)} collective-permute-done((bf16[32,16384]{1,0:T(8,128)(2,1)S(1)}, bf16[32,16384]{1,0:T(8,128)(2,1)S(1)}, u32[]{:S(2)}, u32[]{:S(2)}) %collective-permute-start.5) | collective-permute-done | bytes 1048608 | tf_op jit(solution)/shard_map/ppermute | solution.py:747
  156.7 6.1 %copy.29 = bf16[2,2,2,2,2,32,3072]{6,5,2,3,4,0,1:T(8,128)(2,1)} copy(bf16[2,2,2,2,2,32,3072]{6,5,4,3,2,1,0:T(8,128)(2,1)} %bitcast.99) | data formatting | bytes 12582912 | tf_op jit(solution)/shard_map/reshape | solution.py:658
  163.6 16.4 %mlp.4 = (bf16[16,128,1024]{2,1,0:T(8,128)(2,1)}, bf16[16,128,1024]{2,1,0:T(8,128)(2,1)}, bf16[16,128,1024]{2,1,0:T(8,128)(2,1)}, bf16[16,128,2048]{2,1,0:T(8,12...) custom-call(s32[1]{0:T(128)} %bitcast.refs_0_, ...), custom_call_target="tpu_custom_call" | custom-call | flops 1 | bytes 1 | tf_op jit(solution)/shard_map/mlp/pallas_call | solution.py:67
  180.7 8.8 %collective-permute-done.14.refs_1_ = bf16[16,16384]{1,0:T(8,128)(2,1)S(1)} collective-permute-done((bf16[16,16384]{1,0:T(8,128)(2,1)}, bf16[16,16384]{1,0:T(8,128)(2,1)S(1)}, u32[]{:S(2)}, u32[]{:S(2)}) %collective-permute-start.14) | collective-permute-done | bytes 524320 | tf_op jit(solution)/shard_map/ppermute | solution.py:687
  209.4 16.9 %mlp.5 = (bf16[16,128,1024]{2,1,0:T(8,128)(2,1)}, bf16[16,128,1024]{2,1,0:T(8,128)(2,1)}, bf16[16,128,1024]{2,1,0:T(8,128)(2,1)}, bf16[16,128,2048]{2,1,0:T(8,12...) custom-call(s32[1]{0:T(128)} %bitcast.refs_0_, ...), custom_call_target="tpu_custom_call", output_to_operand_aliasing={{0}: (8, {}), {1}: (9, {}), {2}: (10, {}), {3}: (11, {})} | custom-call | flops 1 | bytes 1 | tf_op jit(solution)/shard_map/mlp/pallas_call | solution.py:67
  257.8 16.6 %mlp.6 = (bf16[16,128,1024]{2,1,0:T(8,128)(2,1)}, bf16[16,128,1024]{2,1,0:T(8,128)(2,1)}, bf16[16,128,1024]{2,1,0:T(8,128)(2,1)}, bf16[16,128,2048]{2,1,0:T(8,12...) custom-call(s32[1]{0:T(128)} %bitcast.refs_0_, ...), custom_call_target="tpu_custom_call", output_to_operand_aliasing={{0}: (8, {}), {1}: (9, {}), {2}: (10, {}), {3}: (11, {})} | custom-call | flops 1 | bytes 1 | tf_op jit(solution)/shard_map/mlp/pallas_call | solution.py:67
  278.6 20.0 %collective-permute-done.23.refs_1_ = bf16[32,16384]{1,0:T(8,128)(2,1)S(1)} collective-permute-done((bf16[32,16384]{1,0:T(8,128)(2,1)S(1)}, bf16[32,16384]{1,0:T(8,128)(2,1)S(1)}, u32[]{:S(2)}, u32[]{:S(2)}) %collective-permute-start.23) | collective-permute-done | bytes 1048608 | tf_op jit(solution)/shard_map/ppermute | solution.py:684
  311.8 10.1 %collective-permute-done.26.refs_2_ = bf16[16,16384]{1,0:T(8,128)(2,1)S(1)} collective-permute-done((bf16[16,16384]{1,0:T(8,128)(2,1)S(1)}, bf16[16,16384]{1,0:T(8,128)(2,1)S(1)}, u32[]{:S(2)}, u32[]{:S(2)}) %collective-permute-start.26) | collective-permute-done | bytes 524320 | tf_op jit(solution)/shard_map/ppermute | solution.py:687
  329.3 17.6 %weight_grad.2 = (bf16[1024,1536]{1,0:T(8,128)(2,1)}, bf16[1024,1536]{1,0:T(8,128)(2,1)}) custom-call(bf16[16,128,1024]{2,1,0:T(8,128)(2,1)} %get-tuple-element.158.refs_0_.refs_9_, bf16[16,128,1024]{2,1,0:T(8,128)(2,1)} %get-tuple-element.159.refs_1_.refs_10_, bf16[16,128,2048]{2,1,0:T(8,128)(2,1)} %get-tuple-element.160.refs_2_.refs_11_, ...), custom_call_target="tpu_custom_call" | custom-call | flops 1 | bytes 1 | tf_op jit(solution)/shard_map/weight_grad/pallas_call | solution.py:67
  347.6 16.4 %mlp.7 = (bf16[16,128,1024]{2,1,0:T(8,128)(2,1)}, bf16[16,128,1024]{2,1,0:T(8,128)(2,1)}, bf16[16,128,1024]{2,1,0:T(8,128)(2,1)}, bf16[16,128,2048]{2,1,0:T(8,12...) custom-call(s32[1]{0:T(128)} %bitcast.refs_0_, ...), custom_call_target="tpu_custom_call", output_to_operand_aliasing={{0}: (8, {}), {1}: (9, {}), {2}: (10, {}), {3}: (11, {})} | custom-call | flops 1 | bytes 1 | tf_op jit(solution)/shard_map/mlp/pallas_call | solution.py:67
  364.6 13.4 %collective-permute-done.29.refs_1_ = bf16[32,16384]{1,0:T(8,128)(2,1)S(1)} collective-permute-done((bf16[32,16384]{1,0:T(8,128)(2,1)S(1)}, bf16[32,16384]{1,0:T(8,128)(2,1)S(1)}, u32[]{:S(2)}, u32[]{:S(2)}) %collective-permute-start.29) | collective-permute-done | bytes 1048608 | tf_op jit(solution)/shard_map/ppermute | solution.py:684
  381.8 12.2 %weight_grad.3 = (bf16[1024,1536]{1,0:T(8,128)(2,1)}, bf16[1024,1536]{1,0:T(8,128)(2,1)}) custom-call(bf16[16,128,1024]{2,1,0:T(8,128)(2,1)} %get-tuple-element.170.refs_0_, bf16[16,128,1024]{2,1,0:T(8,128)(2,1)} %get-tuple-element.171.refs_1_, bf16[16,128,2048]{2,1,0:T(8,128)(2,1)} %get-tuple-element.172.refs_2_, bf16[16,128,1024]{2,1,0:T(8,128)(2,1)} %bitcast.97, ...), custom_call_target="tpu_custom_call" | custom-call | flops 1 | bytes 1 | tf_op jit(solution)/shard_map/weight_grad/pallas_call | solution.py:67
  406.5 12.2 %collective-permute-done.35.refs_2_ = bf16[16,16384]{1,0:T(8,128)(2,1)S(1)} collective-permute-done((bf16[16,16384]{1,0:T(8,128)(2,1)S(1)}, bf16[16,16384]{1,0:T(8,128)(2,1)S(1)}, u32[]{:S(2)}, u32[]{:S(2)}) %collective-permute-start.35) | collective-permute-done | bytes 524320 | tf_op jit(solution)/shard_map/ppermute | solution.py:687
  432.9 18.3 %collective-permute-done.31.refs_1_ = bf16[32,16384]{1,0:T(8,128)(2,1)} collective-permute-done((bf16[32,16384]{1,0:T(8,128)(2,1)S(1)}, bf16[32,16384]{1,0:T(8,128)(2,1)}, u32[]{:S(2)}, u32[]{:S(2)}) %collective-permute-start.31) | collective-permute-done | bytes 1048608 | tf_op jit(solution)/shard_map/ppermute | solution.py:684
  468.6 10.7 %fine_backward.1 = (bf16[16,128,1024]{2,1,0:T(8,128)(2,1)}, f32[16,32,1024]{2,1,0:T(8,128)}, f32[8,96,128]{2,1,0:T(8,128)S(1)}, f32[1,1024]{1,0:T(1,128)S(1)}) custom-call(bf16[16,128,1024]{2,1,0:T(8,128)(2,1)} %bitcast.75, f32[1,1024]{1,0:T(1,128)S(1)} %bitcast.86, bf16[8,128,96]{2,1,0:T(8,128)(2,1)S(1)} %slice.47.refs_2_, ...), custom_call_target="tpu_custom_call" | custom-call | flops 1 | bytes 1 | tf_op jit(solution)/shard_map/fine_backward/pallas_call | solution.py:67
  483.5 7.6 %collective-permute-done.41 = bf16[1280,128]{1,0:T(8,128)(2,1)S(1)} collective-permute-done((bf16[1280,128]{1,0:T(8,128)(2,1)S(1)}, bf16[1280,128]{1,0:T(8,128)(2,1)S(1)}, u32[]{:S(2)}, u32[]{:S(2)}) %collective-permute-start.41) | collective-permute-done | bytes 327712 | tf_op jit(solution)/shard_map/ppermute | solution.py:575
  491.2 16.1 %collective-permute-done.36.refs_2_ = bf16[32,16384]{1,0:T(8,128)(2,1)S(1)} collective-permute-done((bf16[32,16384]{1,0:T(8,128)(2,1)S(1)}, bf16[32,16384]{1,0:T(8,128)(2,1)S(1)}, u32[]{:S(2)}, u32[]{:S(2)}) %collective-permute-start.36) | collective-permute-done | bytes 1048608 | tf_op jit(solution)/shard_map/ppermute | solution.py:757
  511.4 8.0 %collective-permute-done.43.refs_2_ = bf16[4,32,1536]{2,1,0:T(8,128)(2,1)S(1)} collective-permute-done((bf16[4,32,1536]{2,1,0:T(8,128)(2,1)S(1)}, bf16[4,32,1536]{2,1,0:T(8,128)(2,1)S(1)}, u32[]{:S(2)}, u32[]{:S(2)}) %collective-permute-start.43) | collective-permute-done | bytes 393248 | tf_op jit(solution)/shard_map/ppermute | solution.py:636
  531.0 8.9 %collective-permute-done.54 = bf16[1280,128]{1,0:T(8,128)(2,1)S(1)} collective-permute-done((bf16[1280,128]{1,0:T(8,128)(2,1)S(1)}, bf16[1280,128]{1,0:T(8,128)(2,1)S(1)}, u32[]{:S(2)}, u32[]{:S(2)}) %collective-permute-start.54) | collective-permute-done | bytes 327712 | tf_op jit(solution)/shard_map/ppermute | solution.py:575
  544.7 15.3 %collective-permute-done.48 = bf16[1,32,1536]{2,1,0:T(8,128)(2,1)S(1)} collective-permute-done((bf16[1,32,1536]{2,1,0:T(8,128)(2,1)S(1)}, bf16[1,32,1536]{2,1,0:T(8,128)(2,1)S(1)}, u32[]{:S(2)}, u32[]{:S(2)}) %collective-permute-start.48) | collective-permute-done | bytes 98336 | tf_op jit(solution)/shard_map/ppermute | solution.py:636
  (441 shorter events, 225.3 us)
Async XLA Ops:
  41.4 49.8 %collective-permute-start.1 = (bf16[16,49152]{1,0:T(8,128)(2,1)}, bf16[16,49152]{1,0:T(8,128)(2,1)S(1)}, u32[]{:S(2)}, u32[]{:S(2)}) collective-permute-start(bf16[16,49152]{1,0:T(8,128)(2,1)} %get-tuple-element.116.refs_4_), channel_id=1, source_target_pairs={{0,1},{1,0},{2,3},{3,2},{4,5},{5,4},{6,7},{7,6},{8,9},{9,8},{10,11... | collective-permute-start | bytes 4718600 | tf_op jit(solution)/shard_map/ppermute | solution.py:687
  47.0 43.0 %collective-permute-start.3 = (bf16[32,16384]{1,0:T(8,128)(2,1)S(1)}, bf16[32,16384]{1,0:T(8,128)(2,1)S(1)}, u32[]{:S(2)}, u32[]{:S(2)}) collective-permute-start(bf16[32,16384]{1,0:T(8,128)(2,1)S(1)} %stack.8.refs_4_.refs_0_.refs_2_), channel_id=1, source_target_pairs={{0,4},{1,5},{8,12},{9,13},{16,20},{17,21},{24,28},{25,29}} | collective-permute-start | bytes 3145736 | tf_op jit(solution)/shard_map/ppermute | solution.py:747
  52.9 46.7 %collective-permute-start.12 = (bf16[8,32,3072]{2,1,0:T(8,128)(2,1)S(1)}, bf16[8,32,3072]{2,1,0:T(8,128)(2,1)S(1)}, u32[]{:S(2)}, u32[]{:S(2)}) collective-permute-start(bf16[8,32,3072]{2,1,0:T(8,128)(2,1)S(1)} %pad_maximum_fusion.2), channel_id=1, source_target_pairs={{0,16},{8,24},{16,0},{24,8},{1,17},{9,25},{17,1},{25,9},{2,18},{10... | collective-permute-start | bytes 4718600 | tf_op jit(solution)/shard_map/ppermute | solution.py:649
  91.5 46.7 %collective-permute-start.4 = (bf16[32,16384]{1,0:T(8,128)(2,1)S(1)}, bf16[32,16384]{1,0:T(8,128)(2,1)S(1)}, u32[]{:S(2)}, u32[]{:S(2)}) collective-permute-start(bf16[32,16384]{1,0:T(8,128)(2,1)S(1)} %stack.9.refs_0_.refs_4_.refs_2_), channel_id=1, source_target_pairs={{0,2},{1,3},{2,4},{3,5},{4,6},{5,7},{8,10},{9,11},{10,12},{11,13},... | collective-permute-start | bytes 3145736 | tf_op jit(solution)/shard_map/ppermute | solution.py:684
  95.8 42.5 %collective-permute-start.5 = (bf16[32,16384]{1,0:T(8,128)(2,1)S(1)}, bf16[32,16384]{1,0:T(8,128)(2,1)S(1)}, u32[]{:S(2)}, u32[]{:S(2)}) collective-permute-start(bf16[32,16384]{1,0:T(8,128)(2,1)S(1)} %broadcast_select_fusion.9), channel_id=1, source_target_pairs={{0,4},{4,6},{1,5},{5,7},{8,12},{12,14},{9,13},{13,15},{16,20},{20,... | collective-permute-start | bytes 3145736 | tf_op jit(solution)/shard_map/ppermute | solution.py:747
  100.2 49.3 %collective-permute-start.13 = (bf16[16,32,3072]{2,1,0:T(8,128)(2,1)S(1)}, bf16[16,32,3072]{2,1,0:T(8,128)(2,1)S(1)}, u32[]{:S(2)}, u32[]{:S(2)}) collective-permute-start(bf16[16,32,3072]{2,1,0:T(8,128)(2,1)S(1)} %pad_maximum_fusion.1), channel_id=1, source_target_pairs={{0,8},{8,0},{16,24},{24,16},{1,9},{9,1},{17,25},{25,17},{2,10},{10... | collective-permute-start | bytes 9437192 | tf_op jit(solution)/shard_map/ppermute | solution.py:649
  139.9 55.4 %collective-permute-start.6 = (bf16[32,16384]{1,0:T(8,128)(2,1)S(1)}, bf16[32,16384]{1,0:T(8,128)(2,1)S(1)}, u32[]{:S(2)}, u32[]{:S(2)}) collective-permute-start(bf16[32,16384]{1,0:T(8,128)(2,1)S(1)} %stack.10.refs_3_.refs_0_.refs_2_), channel_id=1, source_target_pairs={{0,2},{1,3},{2,4},{3,5},{4,6},{5,7},{8,10},{9,11},{10,12},{11,13},... | collective-permute-start | bytes 3145736 | tf_op jit(solution)/shard_map/ppermute | solution.py:684
  144.1 51.2 %collective-permute-start.7 = (bf16[32,16384]{1,0:T(8,128)(2,1)S(1)}, bf16[32,16384]{1,0:T(8,128)(2,1)S(1)}, u32[]{:S(2)}, u32[]{:S(2)}) collective-permute-start(bf16[32,16384]{1,0:T(8,128)(2,1)S(1)} %broadcast_select_fusion.8), channel_id=1, source_target_pairs={{0,4},{4,6},{1,5},{5,7},{8,12},{12,14},{9,13},{13,15},{16,20},{20,... | collective-permute-start | bytes 3145736 | tf_op jit(solution)/shard_map/ppermute | solution.py:747
  192.3 35.2 %collective-permute-start.17 = (bf16[32,16384]{1,0:T(8,128)(2,1)}, bf16[32,16384]{1,0:T(8,128)(2,1)}, u32[]{:S(2)}, u32[]{:S(2)}) collective-permute-start(bf16[32,16384]{1,0:T(8,128)(2,1)} %stack.11.refs_4_.refs_0_), channel_id=1, source_target_pairs={{2,0},{3,1},{4,2},{5,3},{6,4},{7,5},{10,8},{11,9},{12,10},{13,11},... | collective-permute-start | bytes 3145736 | tf_op jit(solution)/shard_map/ppermute | solution.py:684
  193.6 33.9 %collective-permute-start.20 = (bf16[32,16384]{1,0:T(8,128)(2,1)}, bf16[32,16384]{1,0:T(8,128)(2,1)}, u32[]{:S(2)}, u32[]{:S(2)}) collective-permute-start(bf16[32,16384]{1,0:T(8,128)(2,1)} %stack.11.refs_4_.refs_0_), channel_id=1, source_target_pairs={{6,2},{7,3},{14,10},{15,11},{22,18},{23,19},{30,26},{31,27}} | collective-permute-start | bytes 3145736 | tf_op jit(solution)/shard_map/ppermute | solution.py:757
  201.1 39.7 %collective-permute-start.16 = (bf16[32,16384]{1,0:T(8,128)(2,1)}, bf16[32,16384]{1,0:T(8,128)(2,1)}, u32[]{:S(2)}, u32[]{:S(2)}) collective-permute-start(bf16[32,16384]{1,0:T(8,128)(2,1)} %broadcast_select_fusion.7), channel_id=1, source_target_pairs={{0,4},{4,6},{1,5},{5,7},{8,12},{12,14},{9,13},{13,15},{16,20},{20,... | collective-permute-start | bytes 3145736 | tf_op jit(solution)/shard_map/ppermute | solution.py:747
  205.4 37.5 %collective-permute-start.15 = (bf16[32,16384]{1,0:T(8,128)(2,1)S(1)}, bf16[32,16384]{1,0:T(8,128)(2,1)}, u32[]{:S(2)}, u32[]{:S(2)}) collective-permute-start(bf16[32,16384]{1,0:T(8,128)(2,1)S(1)} %stack.12.refs_3_.refs_0_.refs_2_), channel_id=1, source_target_pairs={{0,2},{1,3},{2,4},{3,5},{4,6},{5,7},{8,10},{9,11},{10,12},{11,13},... | collective-permute-start | bytes 3145736 | tf_op jit(solution)/shard_map/ppermute | solution.py:684
  249.8 28.8 %collective-permute-start.22 = (bf16[32,16384]{1,0:T(8,128)(2,1)}, bf16[32,16384]{1,0:T(8,128)(2,1)S(1)}, u32[]{:S(2)}, u32[]{:S(2)}) collective-permute-start(bf16[32,16384]{1,0:T(8,128)(2,1)} %broadcast_select_fusion.6), channel_id=1, source_target_pairs={{6,2},{2,0},{7,3},{3,1},{14,10},{10,8},{15,11},{11,9},{22,18},{18,... | collective-permute-start | bytes 3145736 | tf_op jit(solution)/shard_map/ppermute | solution.py:757
  251.0 47.6 %collective-permute-start.23 = (bf16[32,16384]{1,0:T(8,128)(2,1)S(1)}, bf16[32,16384]{1,0:T(8,128)(2,1)S(1)}, u32[]{:S(2)}, u32[]{:S(2)}) collective-permute-start(bf16[32,16384]{1,0:T(8,128)(2,1)S(1)} %stack.13.refs_5_.refs_0_), channel_id=1, source_target_pairs={{2,0},{3,1},{4,2},{5,3},{6,4},{7,5},{10,8},{11,9},{12,10},{13,11},... | collective-permute-start | bytes 3145736 | tf_op jit(solution)/shard_map/ppermute | solution.py:684
  275.3 47.7 %collective-permute-start.21 = (bf16[32,16384]{1,0:T(8,128)(2,1)}, bf16[32,16384]{1,0:T(8,128)(2,1)}, u32[]{:S(2)}, u32[]{:S(2)}) collective-permute-start(bf16[32,16384]{1,0:T(8,128)(2,1)} %get-tuple-element.140.refs_3_), channel_id=1, source_target_pairs={{4,6},{5,7},{12,14},{13,15},{20,22},{21,23},{28,30},{29,31}} | collective-permute-start | bytes 3145736 | tf_op jit(solution)/shard_map/ppermute | solution.py:747
  326.6 37.9 %collective-permute-start.30 = (bf16[32,16384]{1,0:T(8,128)(2,1)S(1)}, bf16[32,16384]{1,0:T(8,128)(2,1)S(1)}, u32[]{:S(2)}, u32[]{:S(2)}) collective-permute-start(bf16[32,16384]{1,0:T(8,128)(2,1)S(1)} %broadcast_select_fusion.5), channel_id=1, source_target_pairs={{6,2},{2,0},{7,3},{3,1},{14,10},{10,8},{15,11},{11,9},{22,18},{18,... | collective-permute-start | bytes 3145736 | tf_op jit(solution)/shard_map/ppermute | solution.py:757
  327.9 50.0 %collective-permute-start.29 = (bf16[32,16384]{1,0:T(8,128)(2,1)S(1)}, bf16[32,16384]{1,0:T(8,128)(2,1)S(1)}, u32[]{:S(2)}, u32[]{:S(2)}) collective-permute-start(bf16[32,16384]{1,0:T(8,128)(2,1)S(1)} %stack.14.refs_5_.refs_0_), channel_id=1, source_target_pairs={{2,0},{3,1},{4,2},{5,3},{6,4},{7,5},{10,8},{11,9},{12,10},{13,11},... | collective-permute-start | bytes 3145736 | tf_op jit(solution)/shard_map/ppermute | solution.py:684
  400.2 28.7 %collective-permute-start.32 = (bf16[32,16384]{1,0:T(8,128)(2,1)S(1)}, bf16[32,16384]{1,0:T(8,128)(2,1)S(1)}, u32[]{:S(2)}, u32[]{:S(2)}) collective-permute-start(bf16[32,16384]{1,0:T(8,128)(2,1)S(1)} %broadcast_select_fusion.4), channel_id=1, source_target_pairs={{6,2},{2,0},{7,3},{3,1},{14,10},{10,8},{15,11},{11,9},{22,18},{18,... | collective-permute-start | bytes 3145736 | tf_op jit(solution)/shard_map/ppermute | solution.py:757
  405.2 45.9 %collective-permute-start.31 = (bf16[32,16384]{1,0:T(8,128)(2,1)S(1)}, bf16[32,16384]{1,0:T(8,128)(2,1)}, u32[]{:S(2)}, u32[]{:S(2)}) collective-permute-start(bf16[32,16384]{1,0:T(8,128)(2,1)S(1)} %copy-done.4), channel_id=1, source_target_pairs={{2,0},{3,1},{4,2},{5,3},{6,4},{7,5},{10,8},{11,9},{12,10},{13,11},... | collective-permute-start | bytes 3145736 | tf_op jit(solution)/shard_map/ppermute | solution.py:684
  421.7 38.7 %collective-permute-start.39 = (bf16[8,32,1536]{2,1,0:T(8,128)(2,1)}, bf16[8,32,1536]{2,1,0:T(8,128)(2,1)}, u32[]{:S(2)}, u32[]{:S(2)}) collective-permute-start(bf16[8,32,1536]{2,1,0:T(8,128)(2,1)} %get-tuple-element.183.refs_3_), channel_id=1, source_target_pairs={{0,16},{8,24},{16,0},{24,8},{1,17},{9,25},{17,1},{25,9},{2,18},{10... | collective-permute-start | bytes 2359304 | tf_op jit(solution)/shard_map/ppermute | solution.py:636
  424.3 39.1 %collective-permute-start.38 = (bf16[8,32,1536]{2,1,0:T(8,128)(2,1)}, bf16[8,32,1536]{2,1,0:T(8,128)(2,1)}, u32[]{:S(2)}, u32[]{:S(2)}) collective-permute-start(bf16[8,32,1536]{2,1,0:T(8,128)(2,1)} %get-tuple-element.184.refs_3_), channel_id=1, source_target_pairs={{0,1},{1,0},{2,3},{3,2},{4,5},{5,4},{6,7},{7,6},{8,9},{9,8},{10,11... | collective-permute-start | bytes 2359304 | tf_op jit(solution)/shard_map/ppermute | solution.py:636
  431.8 33.9 %collective-permute-start.37 = (bf16[16,16384]{1,0:T(8,128)(2,1)}, bf16[16,16384]{1,0:T(8,128)(2,1)}, u32[]{:S(2)}, u32[]{:S(2)}) collective-permute-start(bf16[16,16384]{1,0:T(8,128)(2,1)} %get-tuple-element.185.refs_4_), channel_id=1, source_target_pairs={{0,1},{1,0},{2,3},{3,2},{4,5},{5,4},{6,7},{7,6},{8,9},{9,8},{10,11... | collective-permute-start | bytes 1572872 | tf_op jit(solution)/shard_map/ppermute | solution.py:687
  479.5 27.7 %collective-permute-start.36 = (bf16[32,16384]{1,0:T(8,128)(2,1)S(1)}, bf16[32,16384]{1,0:T(8,128)(2,1)S(1)}, u32[]{:S(2)}, u32[]{:S(2)}) collective-permute-start(bf16[32,16384]{1,0:T(8,128)(2,1)S(1)} %copy-done.58), channel_id=1, source_target_pairs={{2,0},{3,1},{10,8},{11,9},{18,16},{19,17},{26,24},{27,25}} | collective-permute-start | bytes 3145736 | tf_op jit(solution)/shard_map/ppermute | solution.py:757
  482.8 28.5 %collective-permute-start.44 = (bf16[4,32,1536]{2,1,0:T(8,128)(2,1)S(1)}, bf16[4,32,1536]{2,1,0:T(8,128)(2,1)S(1)}, u32[]{:S(2)}, u32[]{:S(2)}) collective-permute-start(bf16[4,32,1536]{2,1,0:T(8,128)(2,1)S(1)} %get-tuple-element.197.refs_3_), channel_id=1, source_target_pairs={{0,1},{1,0},{2,3},{3,2},{4,5},{5,4},{6,7},{7,6},{8,9},{9,8},{10,11... | collective-permute-start | bytes 1179656 | tf_op jit(solution)/shard_map/ppermute | solution.py:636
  (152 other events, 1702.2 us)

commit v2 on v1

--- a/solution.py
+++ b/solution.py
@@ -207,28 +207,36 @@
     )
 
 
-def stack_kernel(own, other, out):
-    count = own.shape[0]
-    out[:count] = own[...]
-    out[count:] = other[...]
-
-
-def stack(own, other, unit, at=0):
+def stack_kernel(flag, own, other, *refs):
+    here = jnp.concatenate([own[...], other[...]], axis=0)
+    if len(refs) == 1:
+        refs[0][...] = here
+    else:
+        part, leap, out = refs
+        out[...] = here
+        leap[...] = jnp.where(flag[0] == 1, here, part[...])
+
+
+def stack(flag, own, other, part, unit, at=0):
     blocks, lanes = own.shape
     tile = unit * HALF
     skip = at * lanes // tile
     half = pl.BlockSpec((blocks, tile), lambda t: (0, t))
     taken = pl.BlockSpec((blocks, tile), lambda t: (0, skip + t))
-    return run(
+    whole = pl.BlockSpec((2 * blocks, tile), lambda t: (0, t))
+    shape = jax.ShapeDtypeStruct((2 * blocks, lanes), BF16)
+    more = [] if part is None else [part]
+    outs = run(
         stack_kernel,
         grid=(lanes // tile,),
-        in_specs=[half, taken],
-        out_specs=pl.BlockSpec((2 * blocks, tile), lambda t: (0, t)),
-        out_shape=jax.ShapeDtypeStruct((2 * blocks, lanes), BF16),
-        compiler_params=params(16),
-        operands=[own, other],
+        in_specs=[pl.BlockSpec(memory_space=pltpu.SMEM), half, taken] + [whole] * len(more),
+        out_specs=[whole] * (1 + len(more)),
+        out_shape=[shape] * (1 + len(more)),
+        compiler_params=params(24),
+        operands=[flag, own, other, *more],
         name="stack",
     )
+    return outs[-1], outs[0]
 
 
 def add_kernel(flag, base, extra, own, other):
@@ -390,8 +398,8 @@
     )
 
 
-def weight_kernel(has_prior, mlp_in, active, back_both, cot, *refs):
-    outs, total = refs[-3:-1], refs[-1]
+def weight_kernel(span, bit, mlp_in, active, back_both, cot, *refs):
+    outs, total = refs[:-1], refs[-1]
     count = mlp_in.shape[0] * mlp_in.shape[1]
     step, steps = pl.program_id(0), pl.num_programs(0)
     turn = (((0,), (0,)), ((), ()))
@@ -413,29 +421,32 @@
 
     @pl.when(step == steps - 1)
     def _():
-        for i, out in enumerate(outs):
-            wide = out.shape[1]
-            result = total[:, i * wide:(i + 1) * wide]
-            if has_prior:
-                result = result + refs[i][...].astype(F32)
-            out[...] = result.astype(BF16)
-
-
-def weight_grads_of(kept, cotangent, prior, low, high, unit):
+        for i in range(2):
+            keep, away = outs[2 * i], outs[2 * i + 1]
+            rows, wide = keep.shape
+            columns = slice(i * wide, (i + 1) * wide)
+            for at in range(0, rows, span):
+                mine = pl.multiple_of(2 * at + bit[0] * span, span)
+                theirs = pl.multiple_of(2 * at + (1 - bit[0]) * span, span)
+                keep[at:at + span, :] = total[pl.ds(mine, span), columns].astype(BF16)
+                away[at:at + span, :] = total[pl.ds(theirs, span), columns].astype(BF16)
+
+
+def weight_grads_of(kept, cotangent, bit, inner, devices, unit):
     blocks = cotangent.shape[0]
-    first = low // unit
-    block = pl.BlockSpec((blocks, unit, D), lambda k: (0, first + k, 0))
-    wide = pl.BlockSpec((blocks, unit, 2 * FF), lambda k: (0, first + k, 0))
-    half = pl.BlockSpec((D, 3 * FF // 2), lambda k: (0, 0))
+    block = pl.BlockSpec((blocks, unit, D), lambda k: (0, k, 0))
+    wide = pl.BlockSpec((blocks, unit, 2 * FF), lambda k: (0, k, 0))
+    shape = (D // 2, 3 * FF // 2)
+    half = pl.BlockSpec(shape, lambda k: (0, 0))
     return run(
-        functools.partial(weight_kernel, bool(prior)),
-        grid=((high - low) // unit,),
-        in_specs=[block, block, wide, block] + [half] * len(prior),
-        out_specs=[half, half],
-        out_shape=[jax.ShapeDtypeStruct((D, 3 * FF // 2), BF16)] * 2,
+        functools.partial(weight_kernel, inner * D // devices),
+        grid=(NB // unit,),
+        in_specs=[pl.BlockSpec(memory_space=pltpu.SMEM), block, block, wide, block],
+        out_specs=[half] * 4,
+        out_shape=[jax.ShapeDtypeStruct(shape, BF16)] * 4,
         scratch_shapes=[pltpu.VMEM((D, 3 * FF), F32)],
         compiler_params=params(56),
-        operands=[kept[1], kept[2], kept[3], cotangent, *prior],
+        operands=[bit, kept[1], kept[2], kept[3], cotangent],
         name="weight_grad",
     )
 
@@ -609,7 +620,7 @@
 
 class Scatter:
 
-    def __init__(self, value, late):
+    def __init__(self, late):
         bits = []
         for axis in ("dp", "seq"):
             size = lax.axis_size(axis)
@@ -618,46 +629,89 @@
         inner = [bit for bit in reversed(bits) if bit[0] == "seq"]
         self.order = outer[:1] + inner[:1] + outer[1:] + inner[1:] if late else outer + inner
         self.left = bits
-        self.columns = value.shape[1]
-        self.value = value.reshape(2 ** len(bits), -1, self.columns)
-        self.arriving = None
+        self.next()
+
+    def next(self):
+        self.axis, self.reach = self.order.pop(0)
+        at = self.left.index((self.axis, self.reach))
+        self.left = self.left[:at] + self.left[at + 1:]
+        self.inner = 2 ** (len(self.left) - at)
+        self.bit = ((lax.axis_index(self.axis) // self.reach) % 2).astype(jnp.int32).reshape(1)
+
+    def send(self, keep, away):
+        size = lax.axis_size(self.axis)
+        pairs = [(i, i ^ self.reach) for i in range(size)]
+        self.value, self.arriving = keep, lax.ppermute(away, self.axis, pairs)
 
     def step(self):
         if not self.order:
             self.value, self.arriving = self.value + self.arriving, None
             return
-        axis, reach = self.order.pop(0)
-        at = self.left.index((axis, reach))
-        self.left = self.left[:at] + self.left[at + 1:]
-        inner = 2 ** (len(self.left) - at)
-        size = lax.axis_size(axis)
-        bit = ((lax.axis_index(axis) // reach) % 2).astype(jnp.int32).reshape(1)
-        self.value, away = split(bit, self.value, self.arriving, inner)
-        self.arriving = lax.ppermute(away, axis, [(i, i ^ reach) for i in range(size)])
-
-
-def gather_rows(value):
-    steps = []
-    for axis in ("seq", "dp"):
-        size = lax.axis_size(axis)
-        reaches = [1 << k for k in range(size.bit_length() - 1)]
-        steps += [(axis, reach) for reach in reversed(reaches)]
-    rows, columns = value.shape
-    value = value[None]
-    for axis, reach in steps:
+        self.next()
+        self.send(*split(self.bit, self.value, self.arriving, self.inner))
+
+
+def assemble_kernel(spots, bit, mine, theirs, out):
+    side = bit[0]
+    for j in range(mine.shape[0]):
+        low, high = spots[j]
+        out[low] = jnp.where(side == 0, mine[j], theirs[j])
+        out[high] = jnp.where(side == 0, theirs[j], mine[j])
+
+
+def assemble(bit, mine, theirs, spots):
+    full = lambda shape: pl.BlockSpec(shape, lambda i: (0,) * len(shape))
+    shape = (2 * mine.shape[0],) + mine.shape[1:]
+    return run(
+        functools.partial(assemble_kernel, spots),
+        grid=(1,),
+        in_specs=[pl.BlockSpec(memory_space=pltpu.SMEM), full(mine.shape), full(theirs.shape)],
+        out_specs=full(shape),
+        out_shape=jax.ShapeDtypeStruct(shape, BF16),
+        compiler_params=params(48),
+        operands=[bit, mine, theirs],
+        name="assemble",
+    )
+
+
+class Gather:
+
+    def __init__(self, value):
+        self.steps = []
+        for axis in ("seq", "dp"):
+            size = lax.axis_size(axis)
+            reaches = [1 << k for k in range(size.bit_length() - 1)]
+            self.steps += [(axis, reach) for reach in reversed(reaches)]
+        self.value = value[None]
+        self.at = 0
+        self.send()
+
+    def send(self):
+        axis, reach = self.steps[self.at]
         pairs = [(i, i ^ reach) for i in range(lax.axis_size(axis))]
-        other = lax.ppermute(value, axis, pairs)
-        low = lax.axis_index(axis) // reach % 2 == 0
-        value = jnp.concatenate(
-            [jnp.where(low, value, other), jnp.where(low, other, value)], axis=0
-        )
-    count = len(steps)
-    stepped = list(reversed(steps))
-    wanted = [(axis, 1 << k) for axis in ("dp", "seq")
-              for k in reversed(range(lax.axis_size(axis).bit_length() - 1))]
-    value = value.reshape((2,) * count + (rows, columns))
-    order = [stepped.index(bit) for bit in wanted]
-    return value.transpose(*order, count, count + 1).reshape(-1, columns)
+        self.other = lax.ppermute(self.value, axis, pairs)
+        self.bit = (lax.axis_index(axis) // reach % 2).astype(jnp.int32).reshape(1)
+
+    def step(self):
+        count = self.value.shape[0]
+        self.at += 1
+        if self.at < len(self.steps):
+            spots = [(j, j + count) for j in range(count)]
+            self.value = assemble(self.bit, self.value, self.other, spots)
+            self.send()
+            return
+        seq_bits = lax.axis_size("seq").bit_length() - 1
+        weigh = [reach << (seq_bits if axis == "dp" else 0) for axis, reach in self.steps]
+        spots = []
+        for j in range(count):
+            low = sum(weight for k, weight in enumerate(weigh[:-1]) if j >> k & 1)
+            spots.append((low, low + weigh[-1]))
+        self.value = assemble(self.bit, self.value, self.other, spots)
+
+    def finish(self):
+        while self.at < len(self.steps):
+            self.step()
+        return self.value.reshape(-1, self.value.shape[-1])
 
 
 def on_device(tokens, cotangent, gain_mix, gain_mlp, fine_factor, coarse_factor, w_gate_up, w_down):
@@ -686,7 +740,7 @@
     def swap(value):
         return lax.ppermute(value, "seq", [(i, i ^ 1) for i in range(seq_devices)])
 
-    weights = gather_rows(jnp.concatenate([w_gate_up, w_down], axis=1))
+    gathered = Gather(jnp.concatenate([w_gate_up, w_down], axis=1))
     token_blocks = tokens.reshape(blocks, NB, D)
     cot_blocks = cotangent.reshape(blocks, NB, D)
     row_mix, row_mlp = gain_mix.reshape(1, D), gain_mlp.reshape(1, D)
@@ -736,35 +790,30 @@
     last_flag = (level == depth - 1).astype(jnp.int32).reshape(1)
     first_flag = (level == 0).astype(jnp.int32).reshape(1)
 
-    def jump_up(here, part):
+    def leap_up(value, raw, part):
         pairs = []
         for p in range(planes):
-            if here is not None:
-                pairs.append((p, far * planes + p))
-            if part is not None:
-                pairs.append((far * planes + p, (depth - 1) * planes + p))
-        both = here if part is None else part if here is None else jnp.where(level == 0, here, part)
-        return lax.ppermute(both, "seq", pairs)
-
-    def jump_down(here, part):
+            pairs += [(p, far * planes + p)] if raw else []
+            pairs += [(far * planes + p, (depth - 1) * planes + p)] if part else []
+        return lax.ppermute(value, "seq", pairs)
+
+    def leap_down(value, raw, part):
         pairs = []
         for p in range(planes):
-            if here is not None:
-                pairs.append(((depth - 1) * planes + p, planes + p))
-            if part is not None:
-                pairs.append((planes + p, p))
-        both = here if part is None else part if here is None else jnp.where(level == 1, part, here)
-        return lax.ppermute(both, "seq", pairs)
+            pairs += [((depth - 1) * planes + p, planes + p)] if raw else []
+            pairs += [(planes + p, p)] if part else []
+        return lax.ppermute(value, "seq", pairs)
 
     def stack_up(c):
-        here = part = None
-        if c > 0:
-            part = state[c - 1]["part"]
+        part = state[c - 1]["part"] if c > 0 else None
         if c < count:
-            here = stack(*state[c]["pair"][:2], unit, state[c]["pair"][2])
+            own, other, at = state[c]["pair"]
+            here, leap = stack(first_flag, own, other, part, unit, at)
             middle = [shift(here, d, high=depth - 2) for d in reaches[2:-1]]
             raws = [here, shift(here, 1)] + middle
-        leap = jump_up(here, part)
+        else:
+            leap = part
+        leap = leap_up(leap, c < count, c > 0)
         if c > 0:
             state[c - 1]["extra"] = leap
         if c < count:
@@ -780,7 +829,7 @@
     def run_mlp(c, kept):
         outs = mlp(
             which, token_blocks, cot_blocks, state[c]["own"], state[c]["other"], row_mix, row_mlp,
-            weights, kept, starts[c], unit,
+            gathered.finish(), kept, starts[c], unit,
         )
         names = ["back_after", "mixed", "down_own", "down_other"]
         state[c].update(zip(names, outs[4:8]))
@@ -788,21 +837,27 @@
         state[c]["down_other"] = swap(state[c]["down_other"])
         return list(outs[:4])
 
-    def weight_grad(first, end):
-        sums["weights"] = weight_grads_of(
-            kept, cot_blocks, sums.get("weights", []), starts[end - 1],
-            starts[first] + widths[first], unit,
+    def weight_grad():
+        parts = [Scatter(False), Scatter(True)]
+        first = parts[0]
+        outs = weight_grads_of(
+            kept, cot_blocks, first.bit, first.inner, data_devices * seq_devices, unit
         )
+        for i, part in enumerate(parts):
+            shape = (data_devices * seq_devices // 2, -1, 3 * FF // 2)
+            part.send(outs[2 * i].reshape(shape), outs[2 * i + 1].reshape(shape))
+        return parts
 
     def stack_down(c):
-        here = part = None
-        if c > 0:
-            part = state[c - 1]["part"]
+        part = state[c - 1]["part"] if c > 0 else None
         if c < count:
-            here = stack(state[c]["down_own"], state[c]["down_other"], unit)
+            own, other = state[c]["down_own"], state[c]["down_other"]
+            here, leap = stack(last_flag, own, other, part, unit)
             middle = [shift(here, -d, low=1) for d in reaches[2:-1]]
             backs = [here, shift(here, -1)] + middle
-        leap = jump_down(here, part)
+        else:
+            leap = part
+        leap = leap_down(leap, c < count, c > 0)
         if c > 0:
             state[c - 1]["extra"] = leap
         if c < count:
@@ -826,44 +881,52 @@
         for part in scatters:
             part.step()
 
-    halfway = count - 1
     up_weight = chosen(factor, rows_up, columns_up)
     down_weight = chosen(factor.transpose(0, 2, 1), rows_down, columns_down)
     forward(0)
+    forward(*steps[1:])
     stack_up(0)
-    forward(*steps[1:])
+    while gathered.at < len(gathered.steps) - 3:
+        gathered.step()
     for i in range(count + 1):
+        if i >= 1:
+            add_up(i - 1)
+        if i == 1:
+            Order.also(state[0]["other"])
         if i < count:
             mix_up(i)
             stack_up(i + 1)
+        if i < 2 and gathered.at < len(gathered.steps) - 1:
+            gathered.step()
+        if i >= 3:
+            mix_down(i - 3)
+        if i >= 2:
+            stack_down(i - 2)
+        if i >= 3:
+            factor_grad(i - 3)
+        if i >= 1:
+            kept = run_mlp(i - 1, kept)
         if i >= 4:
-            join_down(i - 4)
-        if i >= 1:
-            add_up(i - 1)
-            if i == count:
-                weight_grad(0, halfway)
-            kept = run_mlp(i - 1, kept)
-        if i >= 2:
-            mix_down(i - 2)
-        if i >= 1:
-            stack_down(i - 1)
-        if i == count:
-            weight_grad(halfway, count)
-            scatters = [Scatter(value, late) for value, late in zip(sums["weights"], (False, True))]
-            scatter_step()
-        if i >= 2:
-            factor_grad(i - 2)
-        if i >= 3:
-            add_down(i - 3)
+            add_down(i - 4)
+    scatters = weight_grad()
+    if count >= 2:
+        mix_down(count - 2)
+    if count >= 3:
+        add_down(count - 3)
+    stack_down(count - 1)
+    if count >= 2:
+        factor_grad(count - 2)
+    if count >= 4:
+        join_down(count - 4)
+    scatter_step()
+    mix_down(count - 1)
+    stack_down(count)
+    if count >= 2:
+        add_down(count - 2)
+    scatter_step()
+    factor_grad(count - 1)
     if count >= 3:
         join_down(count - 3)
-    scatter_step()
-    if count >= 2:
-        add_down(count - 2)
-    mix_down(count - 1)
-    stack_down(count)
-    factor_grad(count - 1)
-    scatter_step()
     if count >= 2:
         join_down(count - 2)
 
@@ -884,11 +947,12 @@
     cut = HG * NC
     joint = jnp.concatenate([placed.reshape(cut, NC), fine_high.astype(BF16).reshape(-1, NB)])
     joint = reduce_all(joint, ("dp",))
-    Order.also(joint)
     add_down(count - 1)
     scatter_step()
+    Order.also(joint)
     joint = reduce_all(joint, ("seq",), first=planes)
     join_down(count - 1)
+    scatter_step()
     fines[0] = state[count - 1]["fine"]
     grad_in, fine_low, gain_low = last(
         token_blocks, row_mix, flipped[:, :width, :width], backs[0], mixes[0], fines[0], rest, grad_in
@@ -913,7 +977,7 @@
     while scatters[0].order or scatters[0].arriving is not None:
         scatter_step()
     weight_grads = jnp.concatenate(
-        [part.value.reshape(-1, part.columns) for part in scatters], axis=1
+        [part.value.reshape(-1, 3 * FF // 2) for part in scatters], axis=1
     ).astype(F32)
     low_rows = small[:-2].reshape(G, width, width)
     low_rows = jnp.pad(low_rows, ((0, 0), (0, 0), (0, NB - width)))

time: 579 us -> 567 us (0.979)
  waiting for transfers between devices: 250 us -> 226 us
  Pallas kernels: 172 us -> 189 us
  other arithmetic: 18.2 us -> 4.06 us
  starting transfers between devices: 78.6 us -> 90.3 us
    pallas_call x52 -> x54, Pallas kernels: 172 us -> 189 us  [run(): pl.pallas_call(body, in_specs=list(in_specs) + [pl.BlockSpec(memory_space...]
    ppermute x15, waiting for transfers between devices: 42.8 us -> 33 us  [swap(): return lax.ppermute(value, 'seq', [(i, i ^ 1) for i in range(seq_devices)])]
    ppermute x25, starting transfers between devices: 41.4 us -> 49.9 us  [the longest x5 23.7 us: leap_up(): return lax.ppermute(value, 'seq', pairs)]
    select_n x11 -> x0, other arithmetic: 6.6 us -> none  [the longest x5 3.94 us: gather_rows(): jnp.where(low, value, other)]
    concatenate x5 -> x0, other arithmetic: 6.58 us -> none  [gather_rows(): jnp.concatenate([jnp.where(low, value, other), jnp.where(low, other, valu...]
    reshape x1 -> x0, local copies, waits for them, and re-layouts: 6.12 us -> none  [gather_rows(): value = value.reshape((2,) * count + (rows, columns))]
    unnamed x239 -> x207, local copies, waits for them, and re-layouts: 41.8 us -> 41.3 us
  transfers between devices with their start and end apart: 57 -> 57, of which waited for: 27 -> 25; matrix products, arithmetic and copies ran while one was open for 4% -> 2% of each run, Pallas kernels for 24% -> 32%
where the time goes in v2:
time: 567 us; the launch traced here: 557 us
  waiting for transfers between devices  226 us (40%)
  Pallas kernels  189 us (33%)
  starting transfers between devices  90.3 us (16%)
  local copies, waits for them, and re-layouts  43.6 us (8%)
    pallas_call x54, Pallas kernels, run(): pl.pallas_call(body, in_specs=list(in_specs) + [pl.BlockSpec(memory_space...  189 us
    ppermute x8, waiting for transfers between devices, shift(): return lax.ppermute(value, 'seq', pairs)  65.3 us
    ppermute x5, waiting for transfers between devices, leap_down(): return lax.ppermute(value, 'seq', pairs)  43 us
    unnamed x207, local copies, waits for them, and re-layouts  41.3 us
    ppermute x5, waiting for transfers between devices, leap_up(): return lax.ppermute(value, 'seq', pairs)  38.1 us
    ppermute x15, waiting for transfers between devices, swap(): return lax.ppermute(value, 'seq', [(i, i ^ 1) for i in range(seq_devices)])  33 us
    ppermute x5, starting transfers between devices, leap_up(): return lax.ppermute(value, 'seq', pairs)  23.7 us
    ppermute x10, waiting for transfers between devices, send(): self.value, self.arriving = (keep, lax.ppermute(away, self.axis, pairs))  22.7 us
  transfers between devices with their start and end apart: 57, of which 25 were waited for; matrix products, arithmetic and copies ran while one was open for 2% of the time, Pallas kernels for 32%

profile of v2, /device:TPU:0, one launch (start us, length us, event | category | flops | bytes accessed | tf_op | source)
XLA Modules:
  0.0 556.9 jit_solution(1626085715794633208)
XLA Ops:
  12.1 10.5 %fine_forward.3 = (bf16[16,16384]{1,0:T(8,128)(2,1)S(1)}, bf16[16,16384]{1,0:T(8,128)(2,1)S(1)}, bf16[16,16384]{1,0:T(8,128)(2,1)S(1)}, bf16[16,49152]{1,0:T(8,128)(2,1)}) custom-call(s32[1]{0:T(128)} %bitcast.refs_0_, bf16[16,128,1024]{2,1,0:T(8,128)(2,1)} %bitcast.65, f32[1,1024]{1,0:T(1,128)S(1)} %bitcast.81, bf16[8,128,128]{2,1,0:T(8,128)(2,1)S(1)} %copy-done.15, ...), custom_call_target="tpu_custom_call" | custom-call | flops 1 | bytes 1 | tf_op jit(solution)/shard_map/fine_forward/pallas_call | solution.py:67
  52.7 18.4 %collective-permute-done.2.refs_1_.refs_3_ = bf16[32,16384]{1,0:T(8,128)(2,1)} collective-permute-done((bf16[32,16384]{1,0:T(8,128)(2,1)S(1)}, bf16[32,16384]{1,0:T(8,128)(2,1)}, u32[]{:S(2)}, u32[]{:S(2)}) %collective-permute-start.2) | collective-permute-done | bytes 1048608 | tf_op jit(solution)/shard_map/ppermute | solution.py:738
  71.1 21.5 %collective-permute-done.3.refs_2_.refs_4_ = bf16[32,16384]{1,0:T(8,128)(2,1)} collective-permute-done((bf16[32,16384]{1,0:T(8,128)(2,1)S(1)}, bf16[32,16384]{1,0:T(8,128)(2,1)}, u32[]{:S(2)}, u32[]{:S(2)}) %collective-permute-start.3) | collective-permute-done | bytes 1048608 | tf_op jit(solution)/shard_map/ppermute | solution.py:798
  96.6 6.4 %collective-permute-start.7 = (bf16[32,16384]{1,0:T(8,128)(2,1)}, bf16[32,16384]{1,0:T(8,128)(2,1)}, u32[]{:S(2)}, u32[]{:S(2)}) collective-permute-start(bf16[32,16384]{1,0:T(8,128)(2,1)} %get-tuple-element.129), channel_id=1, source_target_pairs={{0,4},{4,6},{1,5},{5,7},{8,12},{12,14},{9,13},{13,15},{16,20},{20,... | collective-permute-start | bytes 3145736 | tf_op jit(solution)/shard_map/ppermute | solution.py:798
  109.3 16.6 %collective-permute-done.7.refs_2_.refs_4_ = bf16[32,16384]{1,0:T(8,128)(2,1)} collective-permute-done((bf16[32,16384]{1,0:T(8,128)(2,1)}, bf16[32,16384]{1,0:T(8,128)(2,1)}, u32[]{:S(2)}, u32[]{:S(2)}) %collective-permute-start.7) | collective-permute-done | bytes 1048608 | tf_op jit(solution)/shard_map/ppermute | solution.py:798
  131.6 14.9 %collective-permute-done.6.refs_1_.refs_3_ = bf16[32,16384]{1,0:T(8,128)(2,1)} collective-permute-done((bf16[32,16384]{1,0:T(8,128)(2,1)}, bf16[32,16384]{1,0:T(8,128)(2,1)}, u32[]{:S(2)}, u32[]{:S(2)}) %collective-permute-start.6) | collective-permute-done | bytes 1048608 | tf_op jit(solution)/shard_map/ppermute | solution.py:738
  154.6 6.3 %collective-permute-start.11 = (bf16[32,16384]{1,0:T(8,128)(2,1)}, bf16[32,16384]{1,0:T(8,128)(2,1)}, u32[]{:S(2)}, u32[]{:S(2)}) collective-permute-start(bf16[32,16384]{1,0:T(8,128)(2,1)} %get-tuple-element.134), channel_id=1, source_target_pairs={{0,4},{4,6},{1,5},{5,7},{8,12},{12,14},{9,13},{13,15},{16,20},{20,... | collective-permute-start | bytes 3145736 | tf_op jit(solution)/shard_map/ppermute | solution.py:798
  170.0 16.4 %mlp.4 = (bf16[16,128,1024]{2,1,0:T(8,128)(2,1)}, bf16[16,128,1024]{2,1,0:T(8,128)(2,1)}, bf16[16,128,1024]{2,1,0:T(8,128)(2,1)}, bf16[16,128,2048]{2,1,0:T(8,12...) custom-call(s32[1]{0:T(128)} %bitcast.refs_0_, ...), custom_call_target="tpu_custom_call" | custom-call | flops 1 | bytes 1 | tf_op jit(solution)/shard_map/mlp/pallas_call | solution.py:67
  191.0 14.7 %collective-permute-done.10.refs_1_.refs_3_ = bf16[32,16384]{1,0:T(8,128)(2,1)} collective-permute-done((bf16[32,16384]{1,0:T(8,128)(2,1)}, bf16[32,16384]{1,0:T(8,128)(2,1)}, u32[]{:S(2)}, u32[]{:S(2)}) %collective-permute-start.10) | collective-permute-done | bytes 1048608 | tf_op jit(solution)/shard_map/ppermute | solution.py:738
  221.1 8.0 %collective-permute-done.16.refs_4_ = bf16[16,16384]{1,0:T(8,128)(2,1)S(1)} collective-permute-done((bf16[16,16384]{1,0:T(8,128)(2,1)S(1)}, bf16[16,16384]{1,0:T(8,128)(2,1)S(1)}, u32[]{:S(2)}, u32[]{:S(2)}) %collective-permute-start.16) | collective-permute-done | bytes 524320 | tf_op jit(solution)/shard_map/ppermute | solution.py:741
  229.9 16.6 %mlp.5 = (bf16[16,128,1024]{2,1,0:T(8,128)(2,1)}, bf16[16,128,1024]{2,1,0:T(8,128)(2,1)}, bf16[16,128,1024]{2,1,0:T(8,128)(2,1)}, bf16[16,128,2048]{2,1,0:T(8,12...) custom-call(s32[1]{0:T(128)} %bitcast.refs_0_, ...), custom_call_target="tpu_custom_call", output_to_operand_aliasing={{0}: (8, {}), {1}: (9, {}), {2}: (10, {}), {3}: (11, {})} | custom-call | flops 1 | bytes 1 | tf_op jit(solution)/shard_map/mlp/pallas_call | solution.py:67
  249.4 9.8 %collective-permute-done.14.refs_1_.refs_3_ = bf16[32,16384]{1,0:T(8,128)(2,1)S(1)} collective-permute-done((bf16[32,16384]{1,0:T(8,128)(2,1)S(1)}, bf16[32,16384]{1,0:T(8,128)(2,1)S(1)}, u32[]{:S(2)}, u32[]{:S(2)}) %collective-permute-start.14) | collective-permute-done | bytes 1048608 | tf_op jit(solution)/shard_map/ppermute | solution.py:738
  278.3 16.5 %mlp.6 = (bf16[16,128,1024]{2,1,0:T(8,128)(2,1)}, bf16[16,128,1024]{2,1,0:T(8,128)(2,1)}, bf16[16,128,1024]{2,1,0:T(8,128)(2,1)}, bf16[16,128,2048]{2,1,0:T(8,12...) custom-call(s32[1]{0:T(128)} %bitcast.refs_0_, ...), custom_call_target="tpu_custom_call", output_to_operand_aliasing={{0}: (8, {}), {1}: (9, {}), {2}: (10, {}), {3}: (11, {})} | custom-call | flops 1 | bytes 1 | tf_op jit(solution)/shard_map/mlp/pallas_call | solution.py:67
  299.9 19.6 %collective-permute-done.26.refs_2_ = bf16[32,16384]{1,0:T(8,128)(2,1)S(1)} collective-permute-done((bf16[32,16384]{1,0:T(8,128)(2,1)}, bf16[32,16384]{1,0:T(8,128)(2,1)S(1)}, u32[]{:S(2)}, u32[]{:S(2)}) %collective-permute-start.26) | collective-permute-done | bytes 1048608 | tf_op jit(solution)/shard_map/ppermute | solution.py:805
  330.0 16.4 %mlp.7 = (bf16[16,128,1024]{2,1,0:T(8,128)(2,1)}, bf16[16,128,1024]{2,1,0:T(8,128)(2,1)}, bf16[16,128,1024]{2,1,0:T(8,128)(2,1)}, bf16[16,128,2048]{2,1,0:T(8,12...) custom-call(s32[1]{0:T(128)} %bitcast.refs_0_, ...), custom_call_target="tpu_custom_call", output_to_operand_aliasing={{0}: (8, {}), {1}: (9, {}), {2}: (10, {}), {3}: (11, {})} | custom-call | flops 1 | bytes 1 | tf_op jit(solution)/shard_map/mlp/pallas_call | solution.py:67
  348.4 21.5 %weight_grad.1 = (bf16[512,1536]{1,0:T(8,128)(2,1)}, bf16[512,1536]{1,0:T(8,128)(2,1)}, bf16[512,1536]{1,0:T(8,128)(2,1)}, bf16[512,1536]{1,0:T(8,128)(2,1)}) custom-call(s32[1]{0:T(128)} %bitcast.13.refs_0_, bf16[16,128,1024]{2,1,0:T(8,128)(2,1)} %get-tuple-element.181.refs_1_, bf16[16,128,1024]{2,1,0:T(8,128)(2,1)} %get-tuple-element.182.refs_2_, ...), custom_call_target="tpu_custom_call" | custom-call | flops 1 | bytes 1 | tf_op jit(solution)/shard_map/weight_grad/pallas_call | solution.py:67
  377.3 7.1 %collective-permute-done.27.refs_2_ = bf16[16,16384]{1,0:T(8,128)(2,1)S(1)} collective-permute-done((bf16[16,16384]{1,0:T(8,128)(2,1)S(1)}, bf16[16,16384]{1,0:T(8,128)(2,1)S(1)}, u32[]{:S(2)}, u32[]{:S(2)}) %collective-permute-start.27) | collective-permute-done | bytes 524320 | tf_op jit(solution)/shard_map/ppermute | solution.py:741
  392.7 9.2 %collective-permute-done.34.refs_2_ = bf16[16,16384]{1,0:T(8,128)(2,1)S(1)} collective-permute-done((bf16[16,16384]{1,0:T(8,128)(2,1)S(1)}, bf16[16,16384]{1,0:T(8,128)(2,1)S(1)}, u32[]{:S(2)}, u32[]{:S(2)}) %collective-permute-start.34) | collective-permute-done | bytes 524320 | tf_op jit(solution)/shard_map/ppermute | solution.py:741
  409.7 7.5 %collective-permute-done.30.refs_1_ = bf16[32,16384]{1,0:T(8,128)(2,1)S(1)} collective-permute-done((bf16[32,16384]{1,0:T(8,128)(2,1)S(1)}, bf16[32,16384]{1,0:T(8,128)(2,1)S(1)}, u32[]{:S(2)}, u32[]{:S(2)}) %collective-permute-start.30) | collective-permute-done | bytes 1048608 | tf_op jit(solution)/shard_map/ppermute | solution.py:738
  417.1 21.0 %collective-permute-done.31.refs_2_ = bf16[32,16384]{1,0:T(8,128)(2,1)S(1)} collective-permute-done((bf16[32,16384]{1,0:T(8,128)(2,1)S(1)}, bf16[32,16384]{1,0:T(8,128)(2,1)S(1)}, u32[]{:S(2)}, u32[]{:S(2)}) %collective-permute-start.31) | collective-permute-done | bytes 1048608 | tf_op jit(solution)/shard_map/ppermute | solution.py:805
  467.3 10.6 %fine_backward.1 = (bf16[16,128,1024]{2,1,0:T(8,128)(2,1)}, f32[16,32,1024]{2,1,0:T(8,128)}, f32[8,96,128]{2,1,0:T(8,128)S(1)}, f32[1,1024]{1,0:T(1,128)S(1)}) custom-call(bf16[16,128,1024]{2,1,0:T(8,128)(2,1)} %bitcast.70, f32[1,1024]{1,0:T(1,128)S(1)} %bitcast.82, bf16[8,128,96]{2,1,0:T(8,128)(2,1)S(1)} %copy-done.25, ...), custom_call_target="tpu_custom_call" | custom-call | flops 1 | bytes 1 | tf_op jit(solution)/shard_map/fine_backward/pallas_call | solution.py:67
  485.2 6.5 %collective-permute-done.42.refs_2_ = bf16[4,32,1536]{2,1,0:T(8,128)(2,1)S(1)} collective-permute-done((bf16[4,32,1536]{2,1,0:T(8,128)(2,1)S(1)}, bf16[4,32,1536]{2,1,0:T(8,128)(2,1)S(1)}, u32[]{:S(2)}, u32[]{:S(2)}) %collective-permute-start.42) | collective-permute-done | bytes 393248 | tf_op jit(solution)/shard_map/ppermute | solution.py:644
  511.8 9.8 %collective-permute-done.54 = bf16[1280,128]{1,0:T(8,128)(2,1)S(1)} collective-permute-done((bf16[1280,128]{1,0:T(8,128)(2,1)S(1)}, bf16[1280,128]{1,0:T(8,128)(2,1)S(1)}, u32[]{:S(2)}, u32[]{:S(2)}) %collective-permute-start.54) | collective-permute-done | bytes 327712 | tf_op jit(solution)/shard_map/ppermute | solution.py:586
  526.3 16.0 %collective-permute-done.47 = bf16[1,32,1536]{2,1,0:T(8,128)(2,1)S(1)} collective-permute-done((bf16[1,32,1536]{2,1,0:T(8,128)(2,1)S(1)}, bf16[1,32,1536]{2,1,0:T(8,128)(2,1)S(1)}, u32[]{:S(2)}, u32[]{:S(2)}) %collective-permute-start.47) | collective-permute-done | bytes 98336 | tf_op jit(solution)/shard_map/ppermute | solution.py:644
  (394 shorter events, 233.0 us)
Async XLA Ops:
  25.0 69.9 %collective-permute-start = (bf16[16,49152]{1,0:T(8,128)(2,1)}, bf16[16,49152]{1,0:T(8,128)(2,1)S(1)}, u32[]{:S(2)}, u32[]{:S(2)}) collective-permute-start(bf16[16,49152]{1,0:T(8,128)(2,1)} %get-tuple-element.123.refs_3_), channel_id=1, source_target_pairs={{0,1},{1,0},{2,3},{3,2},{4,5},{5,4},{6,7},{7,6},{8,9},{9,8},{10,11... | collective-permute-start | bytes 4718600 | tf_op jit(solution)/shard_map/ppermute | solution.py:741
  39.2 32.0 %collective-permute-start.2 = (bf16[32,16384]{1,0:T(8,128)(2,1)S(1)}, bf16[32,16384]{1,0:T(8,128)(2,1)}, u32[]{:S(2)}, u32[]{:S(2)}) collective-permute-start(bf16[32,16384]{1,0:T(8,128)(2,1)S(1)} %stack.8.refs_3_.refs_0_.refs_2_), channel_id=1, source_target_pairs={{0,2},{1,3},{2,4},{3,5},{4,6},{5,7},{8,10},{9,11},{10,12},{11,13},... | collective-permute-start | bytes 3145736 | tf_op jit(solution)/shard_map/ppermute | solution.py:738
  43.4 49.3 %collective-permute-start.3 = (bf16[32,16384]{1,0:T(8,128)(2,1)S(1)}, bf16[32,16384]{1,0:T(8,128)(2,1)}, u32[]{:S(2)}, u32[]{:S(2)}) collective-permute-start(bf16[32,16384]{1,0:T(8,128)(2,1)S(1)} %stack.8.refs_3_.refs_0_.refs_2_), channel_id=1, source_target_pairs={{0,4},{1,5},{8,12},{9,13},{16,20},{17,21},{24,28},{25,29}} | collective-permute-start | bytes 3145736 | tf_op jit(solution)/shard_map/ppermute | solution.py:798
  50.6 52.4 %collective-permute-start.8 = (bf16[4,32,3072]{2,1,0:T(8,128)(2,1)}, bf16[4,32,3072]{2,1,0:T(8,128)(2,1)}, u32[]{:S(2)}, u32[]{:S(2)}) collective-permute-start(bf16[4,32,3072]{2,1,0:T(8,128)(2,1)} %assemble.6.refs_4_.refs_1_), channel_id=1, source_target_pairs={{0,1},{1,0},{2,3},{3,2},{4,5},{5,4},{6,7},{7,6},{8,9},{9,8},{10,11... | collective-permute-start | bytes 2359304 | tf_op jit(solution)/shard_map/ppermute | solution.py:692
  105.6 45.2 %collective-permute-start.12 = (bf16[8,32,3072]{2,1,0:T(8,128)(2,1)}, bf16[8,32,3072]{2,1,0:T(8,128)(2,1)}, u32[]{:S(2)}, u32[]{:S(2)}) collective-permute-start(bf16[8,32,3072]{2,1,0:T(8,128)(2,1)} %assemble.7.refs_3_.refs_1_), channel_id=1, source_target_pairs={{0,16},{8,24},{16,0},{24,8},{1,17},{9,25},{17,1},{25,9},{2,18},{10... | collective-permute-start | bytes 4718600 | tf_op jit(solution)/shard_map/ppermute | solution.py:692
  107.1 39.4 %collective-permute-start.6 = (bf16[32,16384]{1,0:T(8,128)(2,1)}, bf16[32,16384]{1,0:T(8,128)(2,1)}, u32[]{:S(2)}, u32[]{:S(2)}) collective-permute-start(bf16[32,16384]{1,0:T(8,128)(2,1)} %get-tuple-element.128.refs_3_.refs_0_.refs_2_), channel_id=1, source_target_pairs={{0,2},{1,3},{2,4},{3,5},{4,6},{5,7},{8,10},{9,11},{10,12},{11,13},... | collective-permute-start | bytes 3145736 | tf_op jit(solution)/shard_map/ppermute | solution.py:738
  154.6 33.5 %collective-permute-start.11 = (bf16[32,16384]{1,0:T(8,128)(2,1)}, bf16[32,16384]{1,0:T(8,128)(2,1)}, u32[]{:S(2)}, u32[]{:S(2)}) collective-permute-start(bf16[32,16384]{1,0:T(8,128)(2,1)} %get-tuple-element.134), channel_id=1, source_target_pairs={{0,4},{4,6},{1,5},{5,7},{8,12},{12,14},{9,13},{13,15},{16,20},{20,... | collective-permute-start | bytes 3145736 | tf_op jit(solution)/shard_map/ppermute | solution.py:798
  160.8 44.9 %collective-permute-start.10 = (bf16[32,16384]{1,0:T(8,128)(2,1)}, bf16[32,16384]{1,0:T(8,128)(2,1)}, u32[]{:S(2)}, u32[]{:S(2)}) collective-permute-start(bf16[32,16384]{1,0:T(8,128)(2,1)} %get-tuple-element.133.refs_3_.refs_0_.refs_2_), channel_id=1, source_target_pairs={{0,2},{1,3},{2,4},{3,5},{4,6},{5,7},{8,10},{9,11},{10,12},{11,13},... | collective-permute-start | bytes 3145736 | tf_op jit(solution)/shard_map/ppermute | solution.py:738
  208.8 39.3 %collective-permute-start.15 = (bf16[32,16384]{1,0:T(8,128)(2,1)S(1)}, bf16[32,16384]{1,0:T(8,128)(2,1)S(1)}, u32[]{:S(2)}, u32[]{:S(2)}) collective-permute-start(bf16[32,16384]{1,0:T(8,128)(2,1)S(1)} %get-tuple-element.141), channel_id=1, source_target_pairs={{0,4},{4,6},{1,5},{5,7},{8,12},{12,14},{9,13},{13,15},{16,20},{20,... | collective-permute-start | bytes 3145736 | tf_op jit(solution)/shard_map/ppermute | solution.py:798
  214.1 45.1 %collective-permute-start.14 = (bf16[32,16384]{1,0:T(8,128)(2,1)S(1)}, bf16[32,16384]{1,0:T(8,128)(2,1)S(1)}, u32[]{:S(2)}, u32[]{:S(2)}) collective-permute-start(bf16[32,16384]{1,0:T(8,128)(2,1)S(1)} %get-tuple-element.140.refs_3_.refs_0_.refs_2_), channel_id=1, source_target_pairs={{0,2},{1,3},{2,4},{3,5},{4,6},{5,7},{8,10},{9,11},{10,12},{11,13},... | collective-permute-start | bytes 3145736 | tf_op jit(solution)/shard_map/ppermute | solution.py:738
  218.1 47.6 %collective-permute-start.20 = (bf16[32,16384]{1,0:T(8,128)(2,1)}, bf16[32,16384]{1,0:T(8,128)(2,1)S(1)}, u32[]{:S(2)}, u32[]{:S(2)}) collective-permute-start(bf16[32,16384]{1,0:T(8,128)(2,1)} %stack.12.refs_12_.refs_0_), channel_id=1, source_target_pairs={{2,0},{3,1},{4,2},{5,3},{6,4},{7,5},{10,8},{11,9},{12,10},{13,11},... | collective-permute-start | bytes 3145736 | tf_op jit(solution)/shard_map/ppermute | solution.py:738
  219.4 46.3 %collective-permute-start.22 = (bf16[32,16384]{1,0:T(8,128)(2,1)}, bf16[32,16384]{1,0:T(8,128)(2,1)}, u32[]{:S(2)}, u32[]{:S(2)}) collective-permute-start(bf16[32,16384]{1,0:T(8,128)(2,1)} %stack.12.refs_12_.refs_0_), channel_id=1, source_target_pairs={{6,2},{7,3},{14,10},{15,11},{22,18},{23,19},{30,26},{31,27}} | collective-permute-start | bytes 3145736 | tf_op jit(solution)/shard_map/ppermute | solution.py:805
  262.1 34.2 %collective-permute-start.18 = (bf16[32,16384]{1,0:T(8,128)(2,1)}, bf16[32,16384]{1,0:T(8,128)(2,1)}, u32[]{:S(2)}, u32[]{:S(2)}) collective-permute-start(bf16[32,16384]{1,0:T(8,128)(2,1)} %get-tuple-element.153.refs_4_), channel_id=1, source_target_pairs={{4,6},{5,7},{12,14},{13,15},{20,22},{21,23},{28,30},{29,31}} | collective-permute-start | bytes 3145736 | tf_op jit(solution)/shard_map/ppermute | solution.py:798
  271.6 47.9 %collective-permute-start.26 = (bf16[32,16384]{1,0:T(8,128)(2,1)}, bf16[32,16384]{1,0:T(8,128)(2,1)S(1)}, u32[]{:S(2)}, u32[]{:S(2)}) collective-permute-start(bf16[32,16384]{1,0:T(8,128)(2,1)} %get-tuple-element.172), channel_id=1, source_target_pairs={{6,2},{2,0},{7,3},{3,1},{14,10},{10,8},{15,11},{11,9},{22,18},{18,... | collective-permute-start | bytes 3145736 | tf_op jit(solution)/shard_map/ppermute | solution.py:805
  322.9 48.0 %collective-permute-start.28 = (bf16[32,16384]{1,0:T(8,128)(2,1)S(1)}, bf16[32,16384]{1,0:T(8,128)(2,1)S(1)}, u32[]{:S(2)}, u32[]{:S(2)}) collective-permute-start(bf16[32,16384]{1,0:T(8,128)(2,1)S(1)} %get-tuple-element.174.refs_5_.refs_0_), channel_id=1, source_target_pairs={{2,0},{3,1},{4,2},{5,3},{6,4},{7,5},{10,8},{11,9},{12,10},{13,11},... | collective-permute-start | bytes 3145736 | tf_op jit(solution)/shard_map/ppermute | solution.py:738
  324.2 49.2 %collective-permute-start.29 = (bf16[32,16384]{1,0:T(8,128)(2,1)}, bf16[32,16384]{1,0:T(8,128)(2,1)S(1)}, u32[]{:S(2)}, u32[]{:S(2)}) collective-permute-start(bf16[32,16384]{1,0:T(8,128)(2,1)} %get-tuple-element.180), channel_id=1, source_target_pairs={{6,2},{2,0},{7,3},{3,1},{14,10},{10,8},{15,11},{11,9},{22,18},{18,... | collective-permute-start | bytes 3145736 | tf_op jit(solution)/shard_map/ppermute | solution.py:805
  369.9 33.0 %collective-permute-start.33 = (bf16[16,32,1536]{2,1,0:T(8,128)(2,1)}, bf16[16,32,1536]{2,1,0:T(8,128)(2,1)S(1)}, u32[]{:S(2)}, u32[]{:S(2)}) collective-permute-start(bf16[16,32,1536]{2,1,0:T(8,128)(2,1)} %bitcast.109), channel_id=1, source_target_pairs={{0,8},{8,0},{16,24},{24,16},{1,9},{9,1},{17,25},{25,17},{2,10},{10... | collective-permute-start | bytes 4718600 | tf_op jit(solution)/shard_map/ppermute | solution.py:644
  369.9 35.8 %collective-permute-start.32 = (bf16[16,32,1536]{2,1,0:T(8,128)(2,1)}, bf16[16,32,1536]{2,1,0:T(8,128)(2,1)S(1)}, u32[]{:S(2)}, u32[]{:S(2)}) collective-permute-start(bf16[16,32,1536]{2,1,0:T(8,128)(2,1)} %bitcast.75), channel_id=1, source_target_pairs={{0,8},{8,0},{16,24},{24,16},{1,9},{9,1},{17,25},{25,17},{2,10},{10... | collective-permute-start | bytes 4718600 | tf_op jit(solution)/shard_map/ppermute | solution.py:644
  386.0 31.1 %collective-permute-start.30 = (bf16[32,16384]{1,0:T(8,128)(2,1)S(1)}, bf16[32,16384]{1,0:T(8,128)(2,1)S(1)}, u32[]{:S(2)}, u32[]{:S(2)}) collective-permute-start(bf16[32,16384]{1,0:T(8,128)(2,1)S(1)} %get-tuple-element.191.refs_5_.refs_0_), channel_id=1, source_target_pairs={{2,0},{3,1},{4,2},{5,3},{6,4},{7,5},{10,8},{11,9},{12,10},{13,11},... | collective-permute-start | bytes 3145736 | tf_op jit(solution)/shard_map/ppermute | solution.py:738
  387.3 50.8 %collective-permute-start.31 = (bf16[32,16384]{1,0:T(8,128)(2,1)S(1)}, bf16[32,16384]{1,0:T(8,128)(2,1)S(1)}, u32[]{:S(2)}, u32[]{:S(2)}) collective-permute-start(bf16[32,16384]{1,0:T(8,128)(2,1)S(1)} %get-tuple-element.192), channel_id=1, source_target_pairs={{6,2},{2,0},{7,3},{3,1},{14,10},{10,8},{15,11},{11,9},{22,18},{18,... | collective-permute-start | bytes 3145736 | tf_op jit(solution)/shard_map/ppermute | solution.py:805
  404.2 42.8 %collective-permute-start.39 = (bf16[8,32,1536]{2,1,0:T(8,128)(2,1)}, bf16[8,32,1536]{2,1,0:T(8,128)(2,1)}, u32[]{:S(2)}, u32[]{:S(2)}) collective-permute-start(bf16[8,32,1536]{2,1,0:T(8,128)(2,1)} %get-tuple-element.197.refs_3_), channel_id=1, source_target_pairs={{0,16},{8,24},{16,0},{24,8},{1,17},{9,25},{17,1},{25,9},{2,18},{10... | collective-permute-start | bytes 2359304 | tf_op jit(solution)/shard_map/ppermute | solution.py:644
  407.6 42.5 %collective-permute-start.38 = (bf16[8,32,1536]{2,1,0:T(8,128)(2,1)}, bf16[8,32,1536]{2,1,0:T(8,128)(2,1)}, u32[]{:S(2)}, u32[]{:S(2)}) collective-permute-start(bf16[8,32,1536]{2,1,0:T(8,128)(2,1)} %get-tuple-element.198.refs_4_), channel_id=1, source_target_pairs={{0,1},{1,0},{2,3},{3,2},{4,5},{5,4},{6,7},{7,6},{8,9},{9,8},{10,11... | collective-permute-start | bytes 2359304 | tf_op jit(solution)/shard_map/ppermute | solution.py:644
  408.2 46.6 %collective-permute-start.37 = (bf16[16,16384]{1,0:T(8,128)(2,1)}, bf16[16,16384]{1,0:T(8,128)(2,1)}, u32[]{:S(2)}, u32[]{:S(2)}) collective-permute-start(bf16[16,16384]{1,0:T(8,128)(2,1)} %get-tuple-element.190.refs_4_), channel_id=1, source_target_pairs={{0,1},{1,0},{2,3},{3,2},{4,5},{5,4},{6,7},{7,6},{8,9},{9,8},{10,11... | collective-permute-start | bytes 1572872 | tf_op jit(solution)/shard_map/ppermute | solution.py:741
  443.6 37.6 %collective-permute-start.35 = (bf16[32,16384]{1,0:T(8,128)(2,1)}, bf16[32,16384]{1,0:T(8,128)(2,1)}, u32[]{:S(2)}, u32[]{:S(2)}) collective-permute-start(bf16[32,16384]{1,0:T(8,128)(2,1)} %get-tuple-element.200.refs_3_), channel_id=1, source_target_pairs={{2,0},{3,1},{10,8},{11,9},{18,16},{19,17},{26,24},{27,25}} | collective-permute-start | bytes 3145736 | tf_op jit(solution)/shard_map/ppermute | solution.py:805
  (136 other events, 1575.6 us)
